TPU v7x, 128 devices: a whole 4x4x4 slice. The times are simulated.
128 devices in a mesh: lon: 8 (over x, core), lat: 16 (over z, y).
Axes of the slice: x: 4, y: 4, z: 4, core: 2. Of those that a mesh axis runs over, the one named last changes fastest.
Arguments:
- tokens: bfloat16 [4, 64, 128, 1024], P(None, 'lon', 'lat'), may hold values from -6 to 6
- cotangent: bfloat16 [4, 64, 128, 1024], P(None, 'lon', 'lat'), may hold values from -6 to 6
- attention_in: bfloat16 [1024, 3072], replicated
- attention_out: bfloat16 [1024, 1024], replicated, may hold values from -0.1875 to 0.1875
- norm_attention: float32 [1024], replicated, may hold values from 0.25 to 1.75
- norm_expert: float32 [1024], replicated, may hold values from 0.25 to 1.75
- expert_up: bfloat16 [32, 1024, 4096], P('lon', None, 'lat'), may hold values from -0.1875 to 0.1875
- expert_down: bfloat16 [32, 4096, 1024], P('lon', 'lat'), may hold values from -0.09375 to 0.09375
- route_gain: float32 [4, 64, 128], P(None, 'lon', 'lat'), may hold values from 0.5 to 2
- assignment: int32 [4, 64, 128], P(None, 'lon', 'lat'), may hold values from 0 to 7, as said below
- slot_index: int32 [4, 64, 128], P(None, 'lon', 'lat'), may hold values from 0 to 15, as said below
Outputs:
- grad_tokens: bfloat16 [4, 64, 128, 1024], P(None, 'lon', 'lat')
- grad_up: float32 [32, 1024, 4096], P('lon', None, 'lat')
- grad_down: float32 [32, 4096, 1024], P('lon', 'lat')
Inputs may be any that keep to these rules, and one draw needn't show every extreme that they name: `assignment`: among the rows of one device and one variable group (8 x 8 cells, aligned blocks), no expert is named more than 16 times, and one is named exactly 16 times. `slot_index`: rows of one device and one variable group that name the same expert have distinct slots.
All inputs are finite; a program needn't handle non-finite values.
Results may differ from a plain program's by a relative error of at most 0.02.
Values may be sent and summed in bfloat16 or wider, within the bound.
No kernel may reach another device: no remote copies, remote signals or barrier semaphores. Data moves between devices by JAX's collectives and lax.ppermute only.
A program may use at most 320 MiB of HBM per device.

v0:
```python
import math

import jax
import jax.numpy as jnp
from jax import lax
from jax.sharding import PartitionSpec as P

HS = 64
EPG = 8
WIN = 8
CAP = 16


EPSILON = 1e-06
TANH_SCALE = math.sqrt(2.0 / math.pi)
CUBIC_COEF = 0.044715
MASKED = -1000000000.0


def shifted(block, axis, distance):
    devices = range(lax.axis_size(axis))
    route = [((i - distance) % len(devices), i) for i in devices]
    return lax.ppermute(block, axis, route)


def gelu_parts(preact):
    argument = TANH_SCALE * (preact + CUBIC_COEF * preact * preact * preact)
    tangent = jnp.tanh(argument)
    activated = 0.5 * preact * (1.0 + tangent)
    derivative = 0.5 * (1.0 + tangent) + 0.5 * preact * (1.0 - tangent * tangent) * TANH_SCALE * (
        1.0 + 3.0 * CUBIC_COEF * preact * preact
    )
    return (activated, derivative)


def norm_rows(grid_field, gain_vec):
    values_f = grid_field.astype(jnp.float32)
    factor = lax.rsqrt(jnp.mean(values_f * values_f, -1, keepdims=True) + EPSILON)
    return values_f * factor * gain_vec


def norm_back(grid_field, gain_vec, grad_in):
    values_f = grid_field.astype(jnp.float32)
    factor = lax.rsqrt(jnp.mean(values_f * values_f, -1, keepdims=True) + EPSILON)
    scaled_grad = grad_in * gain_vec
    inner_mean = jnp.mean(values_f * scaled_grad, -1, keepdims=True)
    return factor * scaled_grad - values_f * factor * factor * factor * inner_mean


def to_windows(grid_field, side):
    groups_n, rows_a, rows_b, features = grid_field.shape
    blocked = grid_field.reshape(groups_n, rows_a // side, side, rows_b // side, side, features)
    return blocked.transpose(0, 1, 3, 2, 4, 5).reshape(-1, side * side, features)


def from_windows(blocks, shape, side):
    groups_n, rows_a, rows_b, features = shape
    blocked = blocks.reshape(groups_n, rows_a // side, rows_b // side, side, side, features)
    return blocked.transpose(0, 1, 3, 2, 4, 5).reshape(shape)


def roll_grid(grid_field, direction, shift_rows):
    lon_rows = grid_field.shape[1]
    lat_rows = grid_field.shape[2]
    border = grid_field[:, :shift_rows] if direction < 0 else grid_field[:, lon_rows - shift_rows :]
    arrived = shifted(border, "lon", direction)
    if direction < 0:
        grid_field = jnp.concatenate([grid_field[:, shift_rows:], arrived], 1)
    else:
        grid_field = jnp.concatenate([arrived, grid_field[:, : lon_rows - shift_rows]], 1)
    border = (
        grid_field[:, :, :shift_rows]
        if direction < 0
        else grid_field[:, :, lat_rows - shift_rows :]
    )
    arrived = shifted(border, "lat", direction)
    if direction < 0:
        grid_field = jnp.concatenate([grid_field[:, :, shift_rows:], arrived], 2)
    else:
        grid_field = jnp.concatenate([arrived, grid_field[:, :, : lat_rows - shift_rows]], 2)
    return grid_field


def attention_forward(rolled, region, weight_in, weight_out, gain_vec):
    normed = norm_rows(rolled, gain_vec).astype(jnp.bfloat16)
    blocks = to_windows(normed, WIN)
    windows_n, window_len, features = blocks.shape
    head_count = features // HS
    projected = jnp.dot(blocks.reshape(-1, features), weight_in, preferred_element_type=jnp.float32)
    projected = projected.astype(jnp.bfloat16).reshape(windows_n, window_len, 3, head_count, HS)
    queries = projected[:, :, 0]
    keyset = projected[:, :, 1]
    valueset = projected[:, :, 2]
    scores = jnp.einsum(
        "wqhe,wkhe->whqk", queries, keyset, preferred_element_type=jnp.float32
    ) * HS ** (-0.5)
    zone_ids = to_windows(region[..., None], WIN)[..., 0]
    allowed = zone_ids[:, None, :, None] == zone_ids[:, None, None, :]
    scores = jnp.where(allowed, scores, MASKED)
    row_max = jnp.max(scores, -1, keepdims=True)
    weights_exp = jnp.exp(scores - row_max)
    prob_full = weights_exp / jnp.sum(weights_exp, -1, keepdims=True)
    prob_low = prob_full.astype(jnp.bfloat16)
    attended = jnp.einsum("whqk,wkhe->wqhe", prob_low, valueset, preferred_element_type=jnp.float32)
    attended = attended.astype(jnp.bfloat16).reshape(-1, features)
    output = jnp.dot(attended, weight_out, preferred_element_type=jnp.float32).astype(jnp.bfloat16)
    output = from_windows(output.reshape(windows_n, window_len, features), rolled.shape, WIN)
    return (output, (queries, keyset, valueset, prob_full, prob_low))


def attention_backward(saved, grad_rolled, rolled, weight_in, weight_out, gain_vec):
    queries, keyset, valueset, prob_full, prob_low = saved
    windows_n = prob_full.shape[0]
    window_len = prob_full.shape[2]
    features = weight_out.shape[0]
    grad_rows = to_windows(grad_rolled, WIN).reshape(-1, features)
    grad_att = jnp.dot(grad_rows, weight_out.T, preferred_element_type=jnp.float32).astype(
        jnp.bfloat16
    )
    grad_att = grad_att.reshape(windows_n, window_len, -1, HS)
    grad_probs = jnp.einsum(
        "wqhe,wkhe->whqk", grad_att, valueset, preferred_element_type=jnp.float32
    )
    grad_values = jnp.einsum(
        "whqk,wqhe->wkhe", prob_low, grad_att, preferred_element_type=jnp.float32
    )
    grad_scores = prob_full * (grad_probs - jnp.sum(prob_full * grad_probs, -1, keepdims=True))
    scaled = (grad_scores * HS ** (-0.5)).astype(jnp.bfloat16)
    grad_queries = jnp.einsum("whqk,wkhe->wqhe", scaled, keyset, preferred_element_type=jnp.float32)
    grad_keys = jnp.einsum("whqk,wqhe->wkhe", scaled, queries, preferred_element_type=jnp.float32)
    stacked = (
        jnp.stack([grad_queries, grad_keys, grad_values], 2)
        .astype(jnp.bfloat16)
        .reshape(-1, 3 * features)
    )
    grad_norm = jnp.dot(stacked, weight_in.T, preferred_element_type=jnp.float32)
    grad_norm = from_windows(grad_norm.reshape(windows_n, window_len, features), rolled.shape, WIN)
    return norm_back(rolled, gain_vec, grad_norm).astype(jnp.bfloat16)


def expert_rows(rows_in, rows_grad, weight_up, weight_down):
    preact = jnp.einsum("erd,edf->erf", rows_in, weight_up, preferred_element_type=jnp.float32)
    activated, derivative = gelu_parts(preact)
    hidden = activated.astype(jnp.bfloat16)
    grad_hidden = jnp.einsum(
        "erd,efd->erf", rows_grad, weight_down, preferred_element_type=jnp.float32
    )
    grad_pre = (grad_hidden * derivative).astype(jnp.bfloat16)
    part_down = jnp.einsum("erf,erd->efd", hidden, rows_grad, preferred_element_type=jnp.float32)
    part_up = jnp.einsum("erd,erf->edf", rows_in, grad_pre, preferred_element_type=jnp.float32)
    returned_part = jnp.einsum(
        "erf,edf->erd", grad_pre, weight_up, preferred_element_type=jnp.float32
    )
    return (part_up, part_down, returned_part)


def body(
    tokens,
    cotangent,
    attention_in,
    attention_out,
    norm_attention,
    norm_expert,
    expert_up,
    expert_down,
    route_gain,
    assignment,
    slot_index,
):
    groups_n, lon_rows, lat_rows, features = tokens.shape
    shift_rows = WIN // 2
    lon_count = lax.axis_size("lon")
    lat_count = lax.axis_size("lat")
    lat_global = lax.axis_index("lat") * lat_rows + jnp.arange(lat_rows, dtype=jnp.int32)
    zone_row = (lat_global >= lat_rows * lat_count - shift_rows).astype(jnp.int32)
    region = jnp.broadcast_to(zone_row[None, None, :], (groups_n, lon_rows, lat_rows))
    rolled = roll_grid(tokens, -1, shift_rows)
    produced, saved = attention_forward(rolled, region, attention_in, attention_out, norm_attention)
    attended = roll_grid(produced, 1, shift_rows)
    middle = (tokens.astype(jnp.float32) + attended.astype(jnp.float32)).astype(jnp.bfloat16)
    normed = norm_rows(middle, norm_expert).astype(jnp.bfloat16)
    grad_out = (route_gain[..., None] * cotangent.astype(jnp.float32)).astype(jnp.bfloat16)
    local_experts = expert_up.shape[0]
    group_ids = jnp.arange(groups_n, dtype=jnp.int32)[:, None, None]
    expert_id = (group_ids * EPG + assignment).reshape(-1)
    owner = expert_id // local_experts
    within = expert_id % local_experts
    target = (within * lon_count + owner) * CAP + slot_index.reshape(-1)
    slot_count = local_experts * lon_count * CAP
    selector = (jnp.arange(slot_count, dtype=jnp.int32)[:, None] == target[None, :]).astype(
        jnp.bfloat16
    )
    send_in = jnp.dot(selector, normed.reshape(-1, features), preferred_element_type=jnp.float32)
    send_in = send_in.astype(jnp.bfloat16).reshape(local_experts, lon_count * CAP, features)
    send_grad = jnp.dot(
        selector, grad_out.reshape(-1, features), preferred_element_type=jnp.float32
    )
    send_grad = send_grad.astype(jnp.bfloat16).reshape(local_experts, lon_count * CAP, features)
    recv_in, recv_grad = (
        lax.all_to_all(send_in, "lon", split_axis=1, concat_axis=1, tiled=True),
        lax.all_to_all(send_grad, "lon", split_axis=1, concat_axis=1, tiled=True),
    )
    part_up, part_down, returned_part = expert_rows(
        lax.all_gather(recv_in, "lat", axis=1, tiled=True),
        lax.all_gather(recv_grad, "lat", axis=1, tiled=True),
        expert_up,
        expert_down,
    )
    summed = lax.psum_scatter(
        returned_part.astype(jnp.bfloat16), "lat", scatter_dimension=1, tiled=True
    )
    returned = lax.all_to_all(summed, "lon", split_axis=1, concat_axis=1, tiled=True)
    grad_normed = jnp.dot(
        selector.T, returned.reshape(-1, features), preferred_element_type=jnp.float32
    )
    grad_normed = grad_normed.reshape(groups_n, lon_rows, lat_rows, features)
    grad_middle = cotangent.astype(jnp.float32) + norm_back(middle, norm_expert, grad_normed)
    grad_middle = grad_middle.astype(jnp.bfloat16)
    grad_rolled = roll_grid(grad_middle, -1, shift_rows)
    branch = attention_backward(
        saved, grad_rolled, rolled, attention_in, attention_out, norm_attention
    )
    branch = roll_grid(branch, 1, shift_rows)
    grad_tokens = (grad_middle.astype(jnp.float32) + branch.astype(jnp.float32)).astype(
        jnp.bfloat16
    )
    return (grad_tokens, part_up, part_down)


def solution(mesh):
    return jax.shard_map(
        body,
        mesh=mesh,
        in_specs=(
            P(None, "lon", "lat", None),
            P(None, "lon", "lat", None),
            P(),
            P(),
            P(),
            P(),
            P("lon", None, "lat"),
            P("lon", "lat", None),
            P(None, "lon", "lat"),
            P(None, "lon", "lat"),
            P(None, "lon", "lat"),
        ),
        out_specs=(P(None, "lon", "lat", None), P("lon", None, "lat"), P("lon", "lat", None)),
        check_vma=False,
    )
```

profile of v0, /device:TPU:1, one launch (start us, length us, event | category | flops | bytes accessed | tf_op | source)
XLA Modules:
  0.0 570.5 jit_solution(15196805218359175276)
XLA Ops:
  7.2 1.2 fusion.90
  8.5 1.4 collective-permute-start
  9.9 5.2 collective-permute-done
  15.3 6.3 %collective-permute-start.1 = (bf16[4,8,4,1024]{3,2,1,0:T(4,128)(2,1)S(1)}, bf16[4,8,4,1024]{3,2,1,0:T(4,128)(2,1)S(1)}, u32[]{:S(2)}, u32[]{:S(2)}) collective-permute-start(bf16[4,8,4,1024]{3,2,1,0:T(4,128)(2,1)S(1)} %get-tuple-element.17), channel_id=1, source_target_pairs={{1,0},{2,1},{3,2},{4,3},{5,4},{6,5},{7,6},{8,7},{9,8},{10,9},{11,1... | collective-permute-start | bytes 786440 | tf_op jit(solution)/shard_map/ppermute | solution.py:23
  21.8 4.5 collective-permute-done.1
  27.8 5.7 %convolution_convert_fusion.1 = bf16[256,3072]{1,0:T(8,128)(2,1)} fusion(bf16[256,1024]{1,0:T(8,128)(2,1)S(1)} %fusion.57, bf16[1024,3072]{1,0:T(8,128)(2,1)} %param.13), kind=kOutput, calls=%fused_computation.20 | convolution fusion | flops 1611399168 | bytes 8388608 | tf_op jit(solution)/shard_map/dot_general | solution.py:89
  33.5 4.8 reshape.180
  38.3 3.8 fusion.86
  42.1 2.0 copy.77
  44.1 4.4 fusion.91
  48.6 3.0 fusion.32
  51.6 1.9 copy.48
  53.5 1.5 reshape.181
  55.0 2.5 convolution_convert_fusion.7
  57.6 1.4 collective-permute-start.2
  59.0 3.3 collective-permute-done.2
  62.9 9.1 %collective-permute-done.3 = bf16[4,8,4,1024]{3,2,1,0:T(4,128)(2,1)} collective-permute-done((bf16[4,8,4,1024]{3,2,1,0:T(4,128)(2,1)S(1)}, bf16[4,8,4,1024]{3,2,1,0:T(4,128)(2,1)}, u32[]{:S(2)}, u32[]{:S(2)}) %collective-permute-start.3) | collective-permute-done | bytes 262176 | tf_op jit(solution)/shard_map/ppermute | solution.py:23
  71.9 1.6 fusion.51
  75.0 23.1 %all_to_all.15 = bf16[4,128,1024]{2,0,1:T(4,128)(2,1)S(1)} all-to-all(bf16[4,128,1024]{2,0,1:T(4,128)(2,1)S(1)} %copy.51), channel_id=1, replica_groups=mesh['lon'=8,'lat'=16] {'lon'}, dimensions={1} | all-to-all | bytes 2097152 | tf_op jit(solution)/shard_map/all_to_all | solution.py:200
  98.1 1.3 copy.52
  99.4 12.4 %all-gather.3.cloned.1.call-start = ((), (), s32[]{:S(2)}) async-start(), calls=%async_computation.4 | async-start | bytes 17825792 | tf_op jit(solution)/shard_map/all_gather | solution.py:205
  113.2 18.5 %all_to_all.16 = bf16[4,128,1024]{2,0,1:T(4,128)(2,1)S(1)} all-to-all(bf16[4,128,1024]{2,0,1:T(4,128)(2,1)S(1)} %copy.49), channel_id=1, replica_groups=mesh['lon'=8,'lat'=16] {'lon'}, dimensions={1} | all-to-all | bytes 2097152 | tf_op jit(solution)/shard_map/all_to_all | solution.py:201
  131.7 1.3 copy.50
  133.1 73.9 %all-gather.5.cloned.1.call-done = bf16[4,2048,1024]{2,1,0:T(8,128)(2,1)} async-done(((bf16[4,128,1024]{2,1,0:T(8,128)(2,1)}), bf16[4,2048,1024]{2,1,0:T(8,128)(2,1)}) %all-gather.5.cloned.1.call-update) | async-done | bytes 16777232 | tf_op jit(solution)/shard_map/all_gather | solution.py:204
  207.0 14.1 %fusion.92 = f32[4,2048,256]{2,1,0:T(8,128)} fusion(bf16[4,2048,1024]{2,1,0:T(8,128)(2,1)} %all-gather.5.cloned.1.call-done, bf16[4,1024,256]{2,1,0:T(8,128)(2,1)S(1)} %copy-done), kind=kOutput, calls=%fused_computation.137 | convolution fusion | flops 4294967296 | bytes 27262976 | tf_op jit(solution)/shard_map/erd,edf->erf/dot_general | solution.py:142
  221.1 99.1 %all-gather.3.cloned.1.call-done = bf16[4,2048,1024]{2,1,0:T(8,128)(2,1)} async-done(((bf16[4,128,1024]{2,1,0:T(8,128)(2,1)}), bf16[4,2048,1024]{2,1,0:T(8,128)(2,1)}) %all-gather.3.cloned.1.call-update) | async-done | bytes 16777232 | tf_op jit(solution)/shard_map/all_gather | solution.py:205
  320.2 14.1 %fusion.8 = bf16[4,2048,256]{2,1,0:T(8,128)(2,1)S(1)} fusion(f32[4,2048,256]{2,1,0:T(8,128)} %fusion.92, bf16[4,2048,1024]{2,1,0:T(8,128)(2,1)} %all-gather.3.cloned.1.call-done, bf16[4,256,1024]{2,1,0:T(8,128)(2,1)} %param.18), kind=kOutput, calls=%fused_computation.11 | convolution fusion | flops 4334813184 | bytes 31457280 | tf_op jit(solution)/shard_map/erd,efd->erf/dot_general | solution.py:145
  334.3 1.9 copy-done.5
  336.2 8.1 %convolution_convert_fusion = bf16[4,2048,1024]{2,1,0:T(8,128)(2,1)} fusion(bf16[4,2048,256]{2,1,0:T(8,128)(2,1)S(1)} %fusion.8, bf16[4,1024,256]{2,1,0:T(8,128)(2,1)S(1)} %copy-done), kind=kOutput, calls=%fused_computation.2 | convolution fusion | flops 4303355904 | bytes 23068672 | tf_op jit(solution)/shard_map/erf,edf->erd/dot_general | solution.py:151
  344.4 110.2 %reduce-scatter.2.cloned.1.call-done = bf16[4,128,1024]{2,1,0:T(8,128)(2,1)} async-done(((bf16[4,2048,1024]{2,1,0:T(8,128)(2,1)}), bf16[4,128,1024]{2,1,0:T(8,128)(2,1)}) %reduce-scatter.2.cloned.1.call-update) | async-done | bytes 1048592 | tf_op jit(solution)/shard_map/reduce_scatter | solution.py:209
  454.6 3.0 copy.53
  457.6 5.2 all-to-all-start.2
  462.9 15.0 %all-to-all-done.2 = bf16[4,128,1024]{2,0,1:T(4,128)(2,1)S(1)} async-done(((bf16[4,128,1024]{2,0,1:T(4,128)(2,1)}), bf16[4,128,1024]{2,0,1:T(4,128)(2,1)S(1)}, u32[]{:S(2)}, u32[]{:S(2)}) %all-to-all-start.2) | async-done | bytes 1048608 | tf_op jit(solution)/shard_map/all_to_all | solution.py:212
  478.8 1.6 fusion.50
  481.3 4.9 collective-permute-done.4
  486.4 2.7 collective-permute-start.5
  489.1 6.0 %collective-permute-done.5 = bf16[4,8,4,1024]{3,2,1,0:T(4,128)(2,1)S(1)} collective-permute-done((bf16[4,8,4,1024]{3,2,1,0:T(4,128)(2,1)S(1)}, bf16[4,8,4,1024]{3,2,1,0:T(4,128)(2,1)S(1)}, u32[]{:S(2)}, u32[]{:S(2)}) %collective-permute-start.5) | collective-permute-done | bytes 262176 | tf_op jit(solution)/shard_map/ppermute | solution.py:23
  496.9 2.0 copy.61
  498.8 3.2 fusion.53
  502.0 1.7 fusion.33
  503.7 5.8 %fusion.37 = bf16[4,64,1,16,64]{1,4,3,0,2:T(8,128)(2,1)} fusion(f32[4,16,64,64]{2,3,1,0:T(8,128)} %fusion.53, bf16[4,64,1,16,64]{4,3,2,1,0:T(8,128)(2,1)} %get-tuple-element.5, f32[4,16,64,64]{2,3,1,0:T(8,128)} %get-tuple-element.21, f32[4,16,64]{2,1,0:T(8,128)S(1)} %get-tuple-element.20), kind=kOutput, calls=%fused_computation.42 | convolution fusion | flops 35655744 | bytes 3162112 | tf_op jit(solution)/shard_map/whqk,wkhe->wqhe/dot_general | solution.py:129
  509.6 5.6 fusion.34
  515.2 4.0 pad_maximum_fusion
  519.1 5.2 copy.63
  524.3 4.1 convert_element_type.123
  528.4 4.8 multiply_reduce_fusion.1
  534.5 15.2 %fusion.11 = f32[4,256,1024]{2,1,0:T(8,128)} fusion(bf16[4,2048,1024]{2,1,0:T(8,128)(2,1)} %all-gather.3.cloned.1.call-done, f32[4,2048,256]{2,1,0:T(8,128)} %fusion.92), kind=kOutput, calls=%fused_computation.15 | convolution fusion | flops 4313841664 | bytes 29360128 | tf_op jit(solution)/shard_map/erf,erd->efd/dot_general | solution.py:149
  550.6 11.9 %fusion.93 = f32[4,1024,256]{2,1,0:T(8,128)} fusion(bf16[4,2048,1024]{2,1,0:T(8,128)(2,1)} %all-gather.5.cloned.1.call-done, bf16[4,2048,256]{2,1,0:T(8,128)(2,1)} %copy-done.5), kind=kOutput, calls=%fused_computation.138 | convolution fusion | flops 4294967296 | bytes 25165824 | tf_op jit(solution)/shard_map/erd,erf->edf/dot_general | solution.py:150
  (83 shorter events, 12.5 us)
Async XLA Ops:
  7.2 199.8 %copy-start = (bf16[4,1024,256]{2,1,0:T(8,128)(2,1)S(1)}, bf16[4,1024,256]{2,1,0:T(8,128)(2,1)}, u32[]{:S(2)}) copy-start(bf16[4,1024,256]{2,1,0:T(8,128)(2,1)} %param.17) | copy-start | bytes 6291460
  7.2 199.8 %all-gather.5.cloned.1.call-start = ((), (), s32[]{:S(2)}) async-start(), calls=%async_computation.5 | async-start | bytes 17825792 | tf_op jit(solution)/shard_map/all_gather | solution.py:204
  8.5 6.7 %collective-permute-start = (bf16[4,4,8,1024]{3,2,1,0:T(8,128)(2,1)S(1)}, bf16[4,4,8,1024]{3,2,1,0:T(8,128)(2,1)S(1)}, u32[]{:S(2)}, u32[]{:S(2)}) collective-permute-start(bf16[4,4,8,1024]{3,2,1,0:T(8,128)(2,1)S(1)} %get-tuple-element.19), channel_id=1, source_target_pairs={{16,0},{32,16},{48,32},{64,48},{80,64},{96,80},{112,96},{0,112},{1... | collective-permute-start | bytes 786440 | tf_op jit(solution)/shard_map/ppermute | solution.py:23
  15.3 10.9 %collective-permute-start.1 = (bf16[4,8,4,1024]{3,2,1,0:T(4,128)(2,1)S(1)}, bf16[4,8,4,1024]{3,2,1,0:T(4,128)(2,1)S(1)}, u32[]{:S(2)}, u32[]{:S(2)}) collective-permute-start(bf16[4,8,4,1024]{3,2,1,0:T(4,128)(2,1)S(1)} %get-tuple-element.17), channel_id=1, source_target_pairs={{1,0},{2,1},{3,2},{4,3},{5,4},{6,5},{7,6},{8,7},{9,8},{10,9},{11,1... | collective-permute-start | bytes 786440 | tf_op jit(solution)/shard_map/ppermute | solution.py:23
  26.3 7.2 %copy-start.6 = (bf16[4,8,4,1024]{3,2,1,0:T(4,128)(2,1)}, bf16[4,8,4,1024]{3,2,1,0:T(4,128)(2,1)S(1)}, u32[]{:S(2)}) copy-start(bf16[4,8,4,1024]{3,2,1,0:T(4,128)(2,1)S(1)} %collective-permute-done.1) | copy-start | bytes 786436
  44.1 4.4 copy-start.2
  53.5 9.1 %copy-start.13 = (s32[4,8,8]{2,1,0:T(8,128)S(1)}, s32[4,8,8]{2,1,0:T(8,128)}, u32[]{:S(2)}) copy-start(s32[4,8,8]{2,1,0:T(8,128)} %param.20) | copy-start | bytes 3076
  53.5 9.1 %copy-start.14 = (s32[4,8,8]{2,1,0:T(8,128)S(1)}, s32[4,8,8]{2,1,0:T(8,128)}, u32[]{:S(2)}) copy-start(s32[4,8,8]{2,1,0:T(8,128)} %param.21) | copy-start | bytes 3076
  55.0 18.5 %copy-start.11 = (f32[1024]{0:T(1024)S(1)}, f32[1024]{0:T(1024)}, u32[]{:S(2)}) copy-start(f32[1024]{0:T(1024)} %param.16) | copy-start | bytes 12292
  57.6 4.7 collective-permute-start.2
  62.5 9.5 %collective-permute-start.3 = (bf16[4,8,4,1024]{3,2,1,0:T(4,128)(2,1)S(1)}, bf16[4,8,4,1024]{3,2,1,0:T(4,128)(2,1)}, u32[]{:S(2)}, u32[]{:S(2)}) collective-permute-start(bf16[4,8,4,1024]{3,2,1,0:T(4,128)(2,1)S(1)} %fusion.70), channel_id=1, source_target_pairs={{15,0},{0,1},{1,2},{2,3},{3,4},{4,5},{5,6},{6,7},{7,8},{8,9},{9,10... | collective-permute-start | bytes 786440 | tf_op jit(solution)/shard_map/ppermute | solution.py:23
  75.0 36.8 %copy-start.8 = (bf16[4,8,8,1024]{3,2,1,0:T(8,128)(2,1)S(1)}, bf16[4,8,8,1024]{3,2,1,0:T(8,128)(2,1)}, u32[]{:S(2)}) copy-start(bf16[4,8,8,1024]{3,2,1,0:T(8,128)(2,1)} %param.12) | copy-start | bytes 1572868
  75.0 36.8 %copy-start.12 = (f32[4,8,8]{2,1,0:T(8,128)S(1)}, f32[4,8,8]{2,1,0:T(8,128)}, u32[]{:S(2)}) copy-start(f32[4,8,8]{2,1,0:T(8,128)} %param.19) | copy-start | bytes 3076
  99.4 220.8 %all-gather.3.cloned.1.call-start = ((), (), s32[]{:S(2)}) async-start(), calls=%async_computation.4 | async-start | bytes 17825792 | tf_op jit(solution)/shard_map/all_gather | solution.py:205
  133.1 321.5 %reduce-scatter.2.cloned.1.call-start = ((), (), s32[]{:S(2)}) async-start(), calls=%async_computation.6 | async-start | bytes 17825792 | tf_op jit(solution)/shard_map/reduce_scatter | solution.py:209
  334.3 1.9 copy-start.5
  457.6 20.3 %all-to-all-start.2 = ((bf16[4,128,1024]{2,0,1:T(4,128)(2,1)}), bf16[4,128,1024]{2,0,1:T(4,128)(2,1)S(1)}, u32[]{:S(2)}, u32[]{:S(2)}) async-start(bf16[4,128,1024]{2,0,1:T(4,128)(2,1)} %copy.53), calls=%async_computation.3 | async-start | bytes 2097152 | tf_op jit(solution)/shard_map/all_to_all | solution.py:212
  478.7 16.6 %copy-start.16 = (bf16[1024,1024]{1,0:T(8,128)(2,1)S(1)}, bf16[1024,1024]{1,0:T(8,128)(2,1)}, u32[]{:S(2)}) copy-start(bf16[1024,1024]{1,0:T(8,128)(2,1)} %param.14) | copy-start | bytes 6291460
  480.4 5.8 %collective-permute-start.4 = (bf16[4,4,8,1024]{3,2,1,0:T(8,128)(2,1)S(1)}, bf16[4,4,8,1024]{3,2,1,0:T(8,128)(2,1)S(1)}, u32[]{:S(2)}, u32[]{:S(2)}) collective-permute-start(bf16[4,4,8,1024]{3,2,1,0:T(8,128)(2,1)S(1)} %get-tuple-element.13), channel_id=1, source_target_pairs={{16,0},{32,16},{48,32},{64,48},{80,64},{96,80},{112,96},{0,112},{1... | collective-permute-start | bytes 786440 | tf_op jit(solution)/shard_map/ppermute | solution.py:23
  486.4 8.7 %collective-permute-start.5 = (bf16[4,8,4,1024]{3,2,1,0:T(4,128)(2,1)S(1)}, bf16[4,8,4,1024]{3,2,1,0:T(4,128)(2,1)S(1)}, u32[]{:S(2)}, u32[]{:S(2)}) collective-permute-start(bf16[4,8,4,1024]{3,2,1,0:T(4,128)(2,1)S(1)} %get-tuple-element.11), channel_id=1, source_target_pairs={{1,0},{2,1},{3,2},{4,3},{5,4},{6,5},{7,6},{8,7},{9,8},{10,9},{11,1... | collective-permute-start | bytes 786440 | tf_op jit(solution)/shard_map/ppermute | solution.py:23
  495.4 3.4 copy-start.3
  498.8 3.2 copy-start.4
  498.8 3.2 copy-start.17
  503.7 5.8 %copy-start.9 = (bf16[4,64,1,16,64]{4,3,2,1,0:T(8,128)(2,1)S(1)}, bf16[4,64,1,16,64]{4,3,2,1,0:T(8,128)(2,1)}, u32[]{:S(2)}) copy-start(bf16[4,64,1,16,64]{4,3,2,1,0:T(8,128)(2,1)} %get-tuple-element.7) | copy-start | bytes 1572868
  509.6 5.6 copy-start.10
  524.3 4.1 copy-start.7
  524.3 4.1 copy-start.15
  533.8 16.0 %collective-permute-start.6 = (bf16[4,4,8,1024]{3,2,1,0:T(8,128)(2,1)S(1)}, bf16[4,4,8,1024]{3,2,1,0:T(8,128)(2,1)S(1)}, u32[]{:S(2)}, u32[]{:S(2)}) collective-permute-start(bf16[4,4,8,1024]{3,2,1,0:T(8,128)(2,1)S(1)} %get-tuple-element.8), channel_id=1, source_target_pairs={{112,0},{0,16},{16,32},{32,48},{48,64},{64,80},{80,96},{96,112},{1... | collective-permute-start | bytes 786440 | tf_op jit(solution)/shard_map/ppermute | solution.py:23
  550.0 12.5 %collective-permute-start.7 = (bf16[4,8,4,1024]{3,2,1,0:T(4,128)(2,1)S(1)}, bf16[4,8,4,1024]{3,2,1,0:T(4,128)(2,1)S(1)}, u32[]{:S(2)}, u32[]{:S(2)}) collective-permute-start(bf16[4,8,4,1024]{3,2,1,0:T(4,128)(2,1)S(1)} %fusion.68), channel_id=1, source_target_pairs={{15,0},{0,1},{1,2},{2,3},{3,4},{4,5},{5,6},{6,7},{7,8},{8,9},{9,10... | collective-permute-start | bytes 786440 | tf_op jit(solution)/shard_map/ppermute | solution.py:23
  550.6 13.0 %copy-start.1 = (bf16[4,1024,256]{2,1,0:T(8,128)(2,1)S(1)}, bf16[4,1024,256]{2,1,0:T(8,128)(2,1)}, u32[]{:S(2)}) copy-start(bf16[4,1024,256]{2,1,0:T(8,128)(2,1)} %param.17) | copy-start | bytes 6291460
Sparse Core Ops, SparseCore 0:
  99.5 107.3 all-gather.4
  209.1 111.0 all-gather.2
  344.5 110.0 reduce-scatter.1
where the time goes:
time: 580 us; the launch traced here: 571 us
  waiting for transfers between devices  331 us (57%)
  matrix products  102 us (18%)
  blocking collectives  41.6 us (7%)
  local copies, waits for them, and re-layouts  37.1 us (6%)
  starting transfers between devices  31.8 us (5%)
  between operations  14.5 us (2%)
  other arithmetic  11.8 us (2%)
    reduce_scatter x1, waiting for transfers between devices, body(): lax.psum_scatter(returned_part.astype(jnp.bfloat16), 'lat', scatter_dimen...  110 us
    all_gather x1, waiting for transfers between devices, body(): lax.all_gather(recv_grad, 'lat', axis=1, tiled=True)  99.1 us
    all_gather x1, waiting for transfers between devices, body(): lax.all_gather(recv_in, 'lat', axis=1, tiled=True)  73.9 us
    ppermute x8, waiting for transfers between devices, shifted(): return lax.ppermute(block, axis, route)  33 us
    all_to_all x1, blocking collectives, body(): lax.all_to_all(send_in, 'lon', split_axis=1, concat_axis=1, tiled=True)  23.1 us
    all_to_all x1, blocking collectives, body(): lax.all_to_all(send_grad, 'lon', split_axis=1, concat_axis=1, tiled=True)  18.5 us
    dot_general x1, matrix products, expert_rows(): jnp.einsum('erf,erd->efd', hidden, rows_grad, preferred_element_type=jnp....  15.2 us
    all_to_all x1, waiting for transfers between devices, body(): lax.all_to_all(summed, 'lon', split_axis=1, concat_axis=1, tiled=True)  15 us
  transfers between devices with their start and end apart: 12, of which 10 were waited for; matrix products, arithmetic and copies ran while one was open for 8% of the time, Pallas kernels for 0%

commit v1 on v0

v1 whole, which is shorter than its diff:
```python
import functools
import math

import jax
import jax.numpy as jnp
from jax import lax
from jax.experimental import pallas as pl
from jax.experimental.pallas import tpu as pltpu
from jax.sharding import PartitionSpec as P

HS = 64
EPG = 8
WIN = 8
EPSILON = 1e-06
TANH_SCALE = math.sqrt(2.0 / math.pi)
CUBIC_COEF = 0.044715
MASKED = -1000000000.0

DIRECTIONS = (1, 4, 3, 12)
PARTS = 4
ROWS = 64
SHARD = 272
TILE = 256
CHUNK = 16
TILE_CHUNKS = 24
TILES = 8
BLOCK = 256
BLOCKS = 20
SPARE = 19 * (BLOCK // CHUNK)
BUFFER = BLOCKS * BLOCK


def cube_masks(part):
    masks = [0]
    for step in range(4):
        direction = DIRECTIONS[(part + step) % 4]
        masks += [m ^ direction for m in masks]
    return masks


def swapped(block, axis, direction):
    return lax.ppermute(block, axis, [(i, i ^ direction) for i in range(lax.axis_size(axis))])


def turned(block, distance):
    devices = lax.axis_size("lon")
    return lax.ppermute(block, "lon", [(i, (i + distance) % devices) for i in range(devices)])


def moved(block, lon_step, lat_step):
    lons, lats = lax.axis_size("lon"), lax.axis_size("lat")
    route = [
        (i * lats + j, (i + lon_step) % lons * lats + (j + lat_step) % lats)
        for i in range(lons)
        for j in range(lats)
    ]
    return lax.ppermute(block, ("lon", "lat"), route)


def gelu_parts(preact):
    argument = TANH_SCALE * (preact + CUBIC_COEF * preact * preact * preact)
    tangent = jnp.tanh(argument)
    activated = 0.5 * preact * (1.0 + tangent)
    derivative = 0.5 * (1.0 + tangent) + 0.5 * preact * (1.0 - tangent * tangent) * TANH_SCALE * (
        1.0 + 3.0 * CUBIC_COEF * preact * preact
    )
    return (activated, derivative)


def norm_rows(field, gain_vec):
    values_f = field.astype(jnp.float32)
    factor = lax.rsqrt(jnp.mean(values_f * values_f, -1, keepdims=True) + EPSILON)
    return values_f * factor * gain_vec


def norm_back(field, gain_vec, grad_in):
    values_f = field.astype(jnp.float32)
    factor = lax.rsqrt(jnp.mean(values_f * values_f, -1, keepdims=True) + EPSILON)
    scaled_grad = grad_in * gain_vec
    inner_mean = jnp.mean(values_f * scaled_grad, -1, keepdims=True)
    return factor * scaled_grad - values_f * factor * factor * factor * inner_mean


def dot_f32(a, b, contract=((1,), (0,))):
    return lax.dot_general(a, b, (contract, ((), ())), preferred_element_type=jnp.float32)


def block_rows(index):
    return pl.ds(pl.multiple_of(index * BLOCK, BLOCK), BLOCK)


def chunk_rows(index):
    return pl.ds(pl.multiple_of(index * CHUNK, CHUNK), CHUNK)


def clear_blocks(buffer, count):
    def clear(b, carry):
        buffer[block_rows(b), :] = jnp.zeros((BLOCK, buffer.shape[1]), buffer.dtype)
        return carry

    lax.fori_loop(0, count, clear, 0)


def compact_tile(t, tile, place_ref, slots_row_ref, buffer):
    spots = lax.broadcasted_iota(jnp.int32, (TILE_CHUNKS * CHUNK, TILE), 0)
    pick = (spots == slots_row_ref[t : t + 1, :]).astype(jnp.bfloat16)
    packed = dot_f32(pick, tile).astype(jnp.bfloat16)
    for q in range(TILE_CHUNKS):
        buffer[chunk_rows(place_ref[t, q]), :] = packed[q * CHUNK : (q + 1) * CHUNK]


def grad_kernel(place_ref, plan_ref, offset_ref, rows_ref, own_ref, other_ref, slots_row_ref,
                packed_ref, hidden_ref, raw, weights, packed, hidden, raw_sem, weight_sem, packed_sem, hidden_sem):
    count = plan_ref[BLOCKS]
    loads = []
    for i in range(4 * TILES):
        start = pl.multiple_of(offset_ref[i], CHUNK)
        loads.append(pltpu.make_async_copy(rows_ref.at[pl.ds(start, ROWS)], raw.at[pl.ds(i * ROWS, ROWS)], raw_sem.at[i]))
    for load in loads:
        load.start()
    weight_loads = [
        pltpu.make_async_copy(own_ref, weights.at[pl.ds(0, 4)], weight_sem.at[0]),
        pltpu.make_async_copy(other_ref, weights.at[pl.ds(4, 4)], weight_sem.at[1]),
    ]
    for load in weight_loads:
        load.start()
    clear_blocks(packed, count)
    for t in range(TILES):
        for load in loads[4 * t : 4 * t + 4]:
            load.wait()
        compact_tile(t, raw[t * TILE : (t + 1) * TILE, :], place_ref, slots_row_ref, packed)
    for load in weight_loads:
        load.wait()

    def stores(b):
        return (
            pltpu.make_async_copy(packed.at[block_rows(b)], packed_ref.at[block_rows(b)], packed_sem.at[b]),
            pltpu.make_async_copy(hidden.at[block_rows(b)], hidden_ref.at[block_rows(b)], hidden_sem.at[b]),
        )

    def step(b, carry):
        weight = weights[plan_ref[b]]
        hidden[block_rows(b), :] = dot_f32(packed[block_rows(b), :], weight, ((1,), (1,)))
        for store in stores(b):
            store.start()
        return carry

    lax.fori_loop(0, count, step, 0)

    def finish(b, carry):
        for store in stores(b):
            store.wait()
        return carry

    lax.fori_loop(0, count, finish, 0)


def grad_side(place, plan, offsets, rows, own, other, slots_row):
    hidden_units = own.shape[1]
    features = own.shape[2]
    any_spec = pl.BlockSpec(memory_space=pl.ANY)
    smem = pl.BlockSpec(memory_space=pltpu.SMEM)
    return pl.pallas_call(
        grad_kernel,
        out_shape=(
            jax.ShapeDtypeStruct((BUFFER, features), jnp.bfloat16),
            jax.ShapeDtypeStruct((BUFFER, hidden_units), jnp.float32),
        ),
        in_specs=[smem, smem, smem, any_spec, any_spec, any_spec, pl.BlockSpec(memory_space=pltpu.VMEM)],
        out_specs=(any_spec, any_spec),
        scratch_shapes=[
            pltpu.VMEM((TILES * TILE, features), jnp.bfloat16),
            pltpu.VMEM((EPG, hidden_units, features), jnp.bfloat16),
            pltpu.VMEM((BUFFER, features), jnp.bfloat16),
            pltpu.VMEM((BUFFER, hidden_units), jnp.float32),
            pltpu.SemaphoreType.DMA((4 * TILES,)),
            pltpu.SemaphoreType.DMA((2,)),
            pltpu.SemaphoreType.DMA((BLOCKS,)),
            pltpu.SemaphoreType.DMA((BLOCKS,)),
        ],
        compiler_params=pltpu.CompilerParams(vmem_limit_bytes=40 * 2**20),
        cost_estimate=pl.CostEstimate(flops=6 * 10**9, bytes_accessed=24 * 2**20, transcendentals=0),
    )(place, plan, offsets, rows, own, other, slots_row)


def expert_kernel(place_ref, plan_ref, rows0_ref, rows1_ref, rows2_ref, rows3_ref, own_ref, other_ref, ghid_ref,
                  slots_row_ref, slots_col_ref,
                  back0_ref, back1_ref, back2_ref, back3_ref, packed_ref, hidden_ref, gpre_ref,
                  raw, weights, ghid, packed, result, hidden, gpre, back, stage,
                  raw_sem, weight_sem, ghid_sem, packed_sem, hidden_sem, gpre_sem, back_sem):
    count = plan_ref[BLOCKS]
    row_refs = (rows0_ref, rows1_ref, rows2_ref, rows3_ref)
    back_refs = (back0_ref, back1_ref, back2_ref, back3_ref)

    def half(t):
        return pl.ds(t % 2 * TILE, TILE)

    loads = [
        pltpu.make_async_copy(row_refs[t // 2].at[half(t)], raw.at[pl.ds(t * TILE, TILE)], raw_sem.at[t])
        for t in range(TILES)
    ]
    for load in loads:
        load.start()
    weight_loads = [
        pltpu.make_async_copy(own_ref, weights.at[pl.ds(0, 4)], weight_sem.at[0]),
        pltpu.make_async_copy(other_ref, weights.at[pl.ds(4, 4)], weight_sem.at[1]),
    ]
    for load in weight_loads:
        load.start()

    def ghid_load(b):
        return pltpu.make_async_copy(ghid_ref.at[block_rows(b)], ghid.at[block_rows(b)], ghid_sem.at[b])

    def begin(b, carry):
        ghid_load(b).start()
        return carry

    lax.fori_loop(0, count, begin, 0)
    clear_blocks(packed, count)
    result[SPARE * CHUNK : (SPARE + 1) * CHUNK, :] = jnp.zeros((CHUNK, result.shape[1]), result.dtype)
    for t in range(TILES):
        loads[t].wait()
        compact_tile(t, raw[t * TILE : (t + 1) * TILE, :], place_ref, slots_row_ref, packed)
    for load in weight_loads:
        load.wait()

    def stores(b):
        return (
            pltpu.make_async_copy(packed.at[block_rows(b)], packed_ref.at[block_rows(b)], packed_sem.at[b]),
            pltpu.make_async_copy(hidden.at[block_rows(b)], hidden_ref.at[block_rows(b)], hidden_sem.at[b]),
            pltpu.make_async_copy(gpre.at[block_rows(b)], gpre_ref.at[block_rows(b)], gpre_sem.at[b]),
        )

    def step(b, carry):
        weight = weights[plan_ref[b]]
        ghid_load(b).wait()
        preact = dot_f32(packed[block_rows(b), :], weight)
        activated, derivative = gelu_parts(preact)
        hidden[block_rows(b), :] = activated.astype(jnp.bfloat16)
        grad_pre = (ghid[block_rows(b), :] * derivative).astype(jnp.bfloat16)
        gpre[block_rows(b), :] = grad_pre
        result[block_rows(b), :] = dot_f32(grad_pre, weight, ((1,), (1,))).astype(jnp.bfloat16)
        for store in stores(b):
            store.start()
        return carry

    lax.fori_loop(0, count, step, 0)

    backs = [
        pltpu.make_async_copy(back.at[pl.ds(t * TILE, TILE)], back_refs[t // 2].at[half(t)], back_sem.at[t])
        for t in range(TILES)
    ]
    spots = lax.broadcasted_iota(jnp.int32, (TILE, TILE_CHUNKS * CHUNK), 1)
    for t in range(TILES):
        for q in range(TILE_CHUNKS):
            stage[q * CHUNK : (q + 1) * CHUNK, :] = result[chunk_rows(place_ref[t, q]), :]
        pick = (spots == slots_col_ref[:, t : t + 1]).astype(jnp.bfloat16)
        back[t * TILE : (t + 1) * TILE, :] = dot_f32(pick, stage[...]).astype(jnp.bfloat16)
        backs[t].start()

    def finish(b, carry):
        for store in stores(b):
            store.wait()
        return carry

    lax.fori_loop(0, count, finish, 0)
    for store in backs:
        store.wait()


def expert_side(place, plan, rows, own, other, ghid, slots_row, slots_col):
    features, hidden_units = own.shape[1:]
    any_spec = pl.BlockSpec(memory_space=pl.ANY)
    smem = pl.BlockSpec(memory_space=pltpu.SMEM)
    vmem = pl.BlockSpec(memory_space=pltpu.VMEM)
    part = jax.ShapeDtypeStruct((2 * TILE, features), jnp.bfloat16)
    small = jax.ShapeDtypeStruct((BUFFER, hidden_units), jnp.bfloat16)
    blocks_sem = pltpu.SemaphoreType.DMA((BLOCKS,))
    tiles_sem = pltpu.SemaphoreType.DMA((TILES,))
    outs = pl.pallas_call(
        expert_kernel,
        out_shape=(part,) * 4 + (jax.ShapeDtypeStruct((BUFFER, features), jnp.bfloat16), small, small),
        in_specs=[smem, smem] + [any_spec] * 7 + [vmem, vmem],
        out_specs=(any_spec,) * 7,
        scratch_shapes=[
            pltpu.VMEM((TILES * TILE, features), jnp.bfloat16),
            pltpu.VMEM((EPG, features, hidden_units), jnp.bfloat16),
            pltpu.VMEM((BUFFER, hidden_units), jnp.float32),
            pltpu.VMEM((BUFFER, features), jnp.bfloat16),
            pltpu.VMEM((BUFFER, features), jnp.bfloat16),
            pltpu.VMEM((BUFFER, hidden_units), jnp.bfloat16),
            pltpu.VMEM((BUFFER, hidden_units), jnp.bfloat16),
            pltpu.VMEM((TILES * TILE, features), jnp.bfloat16),
            pltpu.VMEM((TILE_CHUNKS * CHUNK, features), jnp.bfloat16),
            tiles_sem,
            pltpu.SemaphoreType.DMA((2,)),
            blocks_sem,
            blocks_sem,
            blocks_sem,
            blocks_sem,
            tiles_sem,
        ],
        compiler_params=pltpu.CompilerParams(vmem_limit_bytes=52 * 2**20),
        cost_estimate=pl.CostEstimate(flops=10 * 10**9, bytes_accessed=32 * 2**20, transcendentals=10**6),
    )(place, plan, *rows, own, other, ghid, slots_row, slots_col)
    return (outs[:4], outs[4], outs[5], outs[6])


def weight_kernel(plan_ref, rows_ref, gpre_ref, hidden_ref, grad_ref, *refs):
    before, (up_ref, down_ref) = refs[:-2], refs[-2:]
    b = pl.program_id(0)

    @pl.when(b < plan_ref[BLOCKS])
    def _():
        first = jnp.logical_or(b == 0, plan_ref[b] != plan_ref[jnp.maximum(b - 1, 0)])

        @pl.when(first)
        def _():
            if before:
                up_ref[...] = before[0][...]
                down_ref[...] = before[1][...]
            else:
                up_ref[...] = jnp.zeros_like(up_ref)
                down_ref[...] = jnp.zeros_like(down_ref)

        up_ref[0] += dot_f32(rows_ref[...], gpre_ref[...], ((0,), (0,)))
        down_ref[0] += dot_f32(hidden_ref[...], grad_ref[...], ((0,), (0,)))


def weight_side(plan, rows, gpre, hidden, grads, before):
    features, hidden_units = rows.shape[1], hidden.shape[1]

    def at_block(b, plan_ref):
        return (jnp.minimum(b, plan_ref[BLOCKS] - 1), 0)

    def at_expert(b, plan_ref):
        return (plan_ref[jnp.minimum(b, plan_ref[BLOCKS] - 1)], 0, 0)

    up_spec = pl.BlockSpec((1, features, hidden_units), at_expert)
    down_spec = pl.BlockSpec((1, hidden_units, features), at_expert)
    return pl.pallas_call(
        weight_kernel,
        out_shape=(
            jax.ShapeDtypeStruct((EPG, features, hidden_units), jnp.float32),
            jax.ShapeDtypeStruct((EPG, hidden_units, features), jnp.float32),
        ),
        grid_spec=pltpu.PrefetchScalarGridSpec(
            num_scalar_prefetch=1,
            grid=(BLOCKS,),
            in_specs=[
                pl.BlockSpec((BLOCK, features), at_block),
                pl.BlockSpec((BLOCK, hidden_units), at_block),
                pl.BlockSpec((BLOCK, hidden_units), at_block),
                pl.BlockSpec((BLOCK, features), at_block),
            ]
            + ([up_spec, down_spec] if before else []),
            out_specs=(up_spec, down_spec),
        ),
        compiler_params=pltpu.CompilerParams(vmem_limit_bytes=32 * 2**20),
        cost_estimate=pl.CostEstimate(flops=4 * 10**9, bytes_accessed=32 * 2**20, transcendentals=0),
    )(plan, rows, gpre, hidden, grads, *before)


def routes(named):
    onehot = (named[..., None] == jnp.arange(EPG)).astype(jnp.bfloat16)
    earlier = jnp.tril(jnp.ones((TILE, TILE), jnp.bfloat16), -1)
    ranks = jnp.einsum("rs,tse->tre", earlier, onehot, preferred_element_type=jnp.float32)
    onehot_f = onehot.astype(jnp.float32)
    rank = jnp.sum(ranks * onehot_f, -1).astype(jnp.int32)
    counts = jnp.sum(onehot_f, 1).astype(jnp.int32)
    chunks = (counts + CHUNK - 1) // CHUNK

    def before(values, axis):
        return jnp.cumsum(values, axis) - values

    starts = before(chunks, 1)
    slots = CHUNK * jnp.sum(onehot_f * starts[:, None, :].astype(jnp.float32), -1).astype(jnp.int32) + rank
    per_block = BLOCK // CHUNK
    blocks = jnp.maximum((jnp.sum(chunks, 0) + per_block - 1) // per_block, 1)
    first_block = before(blocks, 0)
    places = first_block[None, :] * per_block + before(chunks, 0)
    index = jnp.arange(TILE_CHUNKS)[None, :, None]
    inside = (index >= starts[:, None, :]) & (index < (starts + chunks)[:, None, :])
    place = jnp.sum(jnp.where(inside, places[:, None, :] + index - starts[:, None, :] - SPARE, 0), -1) + SPARE
    number = jnp.arange(BLOCKS)[:, None]
    plan = jnp.sum((number >= first_block[None, :]).astype(jnp.int32), -1) - 1
    plan = jnp.concatenate([plan, jnp.sum(blocks)[None]]).astype(jnp.int32)
    return (place.astype(jnp.int32), plan, slots, slots.T)


def attention_forward(rolled, zone_ids, weight_in, weight_out, gain_vec):
    normed = norm_rows(rolled, gain_vec).astype(jnp.bfloat16)
    windows_n, window_len, features = normed.shape
    head_count = features // HS
    projected = jnp.dot(normed.reshape(-1, features), weight_in, preferred_element_type=jnp.float32)
    projected = projected.astype(jnp.bfloat16).reshape(windows_n, window_len, 3, head_count, HS)
    queries = projected[:, :, 0]
    keyset = projected[:, :, 1]
    valueset = projected[:, :, 2]
    scores = jnp.einsum(
        "wqhe,wkhe->whqk", queries, keyset, preferred_element_type=jnp.float32
    ) * HS ** (-0.5)
    allowed = zone_ids[:, None] == zone_ids[None, :]
    scores = jnp.where(allowed, scores, MASKED)
    row_max = jnp.max(scores, -1, keepdims=True)
    weights_exp = jnp.exp(scores - row_max)
    prob_full = weights_exp / jnp.sum(weights_exp, -1, keepdims=True)
    prob_low = prob_full.astype(jnp.bfloat16)
    attended = jnp.einsum("whqk,wkhe->wqhe", prob_low, valueset, preferred_element_type=jnp.float32)
    attended = attended.astype(jnp.bfloat16).reshape(-1, features)
    output = jnp.dot(attended, weight_out, preferred_element_type=jnp.float32).astype(jnp.bfloat16)
    return (output.reshape(rolled.shape), (queries, keyset, valueset, prob_full, prob_low))


def attention_backward(saved, grad_rolled, rolled, weight_in, weight_out, gain_vec):
    queries, keyset, valueset, prob_full, prob_low = saved
    windows_n = prob_full.shape[0]
    window_len = prob_full.shape[2]
    features = weight_out.shape[0]
    grad_rows = grad_rolled.reshape(-1, features)
    grad_att = jnp.dot(grad_rows, weight_out.T, preferred_element_type=jnp.float32).astype(
        jnp.bfloat16
    )
    grad_att = grad_att.reshape(windows_n, window_len, -1, HS)
    grad_probs = jnp.einsum(
        "wqhe,wkhe->whqk", grad_att, valueset, preferred_element_type=jnp.float32
    )
    grad_values = jnp.einsum(
        "whqk,wqhe->wkhe", prob_low, grad_att, preferred_element_type=jnp.float32
    )
    grad_scores = prob_full * (grad_probs - jnp.sum(prob_full * grad_probs, -1, keepdims=True))
    scaled = (grad_scores * HS ** (-0.5)).astype(jnp.bfloat16)
    grad_queries = jnp.einsum("whqk,wkhe->wqhe", scaled, keyset, preferred_element_type=jnp.float32)
    grad_keys = jnp.einsum("whqk,wqhe->wkhe", scaled, queries, preferred_element_type=jnp.float32)
    stacked = (
        jnp.stack([grad_queries, grad_keys, grad_values], 2)
        .astype(jnp.bfloat16)
        .reshape(-1, 3 * features)
    )
    grad_norm = jnp.dot(stacked, weight_in.T, preferred_element_type=jnp.float32)
    return norm_back(rolled, gain_vec, grad_norm.reshape(rolled.shape)).astype(jnp.bfloat16)


def quadrants(field):
    half = WIN // 2
    cut = lambda a: a.reshape(a.shape[0], half * half, a.shape[-1])
    return (
        cut(field[:, half:, half:]),
        cut(field[:, half:, :half]),
        cut(field[:, :half, half:]),
        cut(field[:, :half, :half]),
    )


def roll_in(field):
    stays, lat_part, lon_part, both = quadrants(field)
    return jnp.concatenate(
        [stays, moved(lat_part, 0, -1), moved(lon_part, -1, 0), moved(both, -1, -1)], 1
    )


def roll_out(field):
    half = WIN // 2
    cells = half * half
    pieces = [field[:, i * cells : (i + 1) * cells] for i in range(4)]
    lat_part, lon_part, both = moved(pieces[1], 0, 1), moved(pieces[2], 1, 0), moved(pieces[3], 1, 1)
    shape = (field.shape[0], half, half, field.shape[-1])
    grid = lambda a: a.reshape(shape)
    upper = jnp.concatenate([grid(both), grid(lon_part)], 2)
    lower = jnp.concatenate([grid(lat_part), grid(pieces[0])], 2)
    return jnp.concatenate([upper, lower], 1)


def to_groups(blocks, place):
    out = [lax.dynamic_index_in_dim(blocks, place, 0, keepdims=False)]
    for k in range(1, PARTS):
        block = lax.dynamic_index_in_dim(blocks, (place + k) % PARTS, 0, keepdims=False)
        out.append(turned(block, 2 * k))
    return out


def cube_gather(parts):
    held = list(parts)
    for step in range(4):
        came = [swapped(held[p], "lat", DIRECTIONS[(p + step) % 4]) for p in range(PARTS)]
        if step == 3:
            return (held, came)
        held = [jnp.concatenate([held[p], came[p]], 0) for p in range(PARTS)]


def cube_sum(kept, sent):
    held = kept
    for step in range(3, -1, -1):
        came = [swapped(sent[p], "lat", DIRECTIONS[(p + step) % 4]) for p in range(PARTS)]
        total = [
            (held[p].astype(jnp.float32) + came[p].astype(jnp.float32)).astype(jnp.bfloat16)
            for p in range(PARTS)
        ]
        half = total[0].shape[0] // 2
        if step == 0:
            return total
        held = [t[:half] for t in total]
        sent = [t[half:] for t in total]


def body(
    tokens,
    cotangent,
    attention_in,
    attention_out,
    norm_attention,
    norm_expert,
    expert_up,
    expert_down,
    route_gain,
    assignment,
    slot_index,
):
    groups_n, lon_rows, lat_rows, features = tokens.shape
    lat_count = lax.axis_size("lat")
    lon_index = lax.axis_index("lon")
    lat_index = lax.axis_index("lat")
    place, core = lon_index // 2, lon_index % 2

    grad_out = (route_gain[..., None] * cotangent.astype(jnp.float32)).astype(jnp.bfloat16)
    named = jnp.transpose(assignment, (1, 2, 0)).astype(jnp.bfloat16)
    named = jnp.pad(named, ((0, 0), (0, 0), (0, features - groups_n)))
    everything = roll_in(jnp.concatenate([tokens, grad_out, named[None]], 0))
    rolled, grad_rows = everything[:groups_n], everything[groups_n : 2 * groups_n]
    named = everything[2 * groups_n][:, :groups_n].T
    named = jnp.pad(named[:, None, :], ((0, 0), (0, CHUNK - 1), (0, features - ROWS)))
    other_down = swapped(expert_down, "lon", 1)
    other_up = swapped(expert_up, "lon", 1)

    came = to_groups(jnp.concatenate([grad_rows, named], 1), place)
    shard = jnp.concatenate(
        [c[:ROWS] for c in came]
        + [c[ROWS : ROWS + 1] for c in came]
        + [jnp.zeros((SHARD - PARTS * (ROWS + 1), features), jnp.bfloat16)],
        0,
    )
    all_grads = lax.all_gather(shard, "lat", axis=0, tiled=True)

    zone_ids = ((jnp.arange(ROWS) // 16 % 2 == 1) & (lat_index == lat_count - 1)).astype(jnp.int32)
    produced, saved = attention_forward(
        rolled, zone_ids, attention_in, attention_out, norm_attention
    )
    middle = (rolled.astype(jnp.float32) + produced.astype(jnp.float32)).astype(jnp.bfloat16)
    normed = norm_rows(middle, norm_expert).astype(jnp.bfloat16)
    kept, late = cube_gather(to_groups(normed, place))

    cotangent = roll_in(cotangent)

    numbers = all_grads.reshape(lat_count, SHARD, features)[:, PARTS * ROWS : PARTS * (ROWS + 1), :ROWS]
    numbers = numbers.astype(jnp.int32) ^ (4 * core)
    masks = jnp.array([cube_masks(p) for p in range(PARTS)], jnp.int32)
    sources = lat_index ^ masks
    picked = (sources[..., None] == jnp.arange(lat_count)).astype(jnp.float32)
    numbers = jnp.einsum("pkj,jpr->pkr", picked, numbers.astype(jnp.float32)).astype(jnp.int32)
    offsets = sources * SHARD + ROWS * jnp.arange(PARTS)[:, None]

    halves = []
    for h, rows in ((0, kept), (1, late)):
        plan = routes(numbers[:, 8 * h : 8 * h + 8].reshape(TILES, TILE))
        spots, blocks, slots, slots_t = plan
        packed_grad, grad_hidden = grad_side(
            spots, blocks, offsets[:, 8 * h : 8 * h + 8].reshape(-1), all_grads, expert_down, other_down, slots
        )
        back, packed, hidden, grad_pre = expert_side(
            spots, blocks, rows, expert_up, other_up, grad_hidden, slots, slots_t
        )
        halves.append((back, blocks, packed, grad_pre, hidden, packed_grad))
    summed = cube_sum(halves[0][0], halves[1][0])
    weight_grads = ()
    for half in halves:
        weight_grads = weight_side(*half[1:], weight_grads)
    up_all, down_all = weight_grads
    grad_up = up_all[:4] + swapped(up_all[4:], "lon", 1)
    grad_down = down_all[:4] + swapped(down_all[4:], "lon", 1)

    returned = [summed[0]] + [turned(summed[k], -2 * k) for k in range(1, PARTS)]
    returned = jnp.roll(jnp.stack(returned), place, 0)
    grad_middle = cotangent.astype(jnp.float32) + norm_back(
        middle, norm_expert, returned.astype(jnp.float32)
    )
    grad_middle = grad_middle.astype(jnp.bfloat16)
    branch = attention_backward(
        saved, grad_middle, rolled, attention_in, attention_out, norm_attention
    )
    grad_tokens = (grad_middle.astype(jnp.float32) + branch.astype(jnp.float32)).astype(
        jnp.bfloat16
    )
    return (roll_out(grad_tokens), grad_up, grad_down)


def solution(mesh):
    return jax.shard_map(
        body,
        mesh=mesh,
        in_specs=(
            P(None, "lon", "lat", None),
            P(None, "lon", "lat", None),
            P(),
            P(),
            P(),
            P(),
            P("lon", None, "lat"),
            P("lon", "lat", None),
            P(None, "lon", "lat"),
            P(None, "lon", "lat"),
            P(None, "lon", "lat"),
        ),
        out_specs=(P(None, "lon", "lat", None), P("lon", None, "lat"), P("lon", "lat", None)),
        check_vma=False,
    )
```

time: 580 us -> 482 us (0.83)
  waiting for transfers between devices: 331 us -> 119 us
  Pallas kernels: 0 us -> 105 us
  matrix products: 102 us -> 40.6 us
  local copies, waits for them, and re-layouts: 37.1 us -> 97.4 us
  blocking collectives: 41.6 us -> 0 us
  starting transfers between devices: 31.8 us -> 62.7 us
  other arithmetic: 11.8 us -> 35.4 us
    all_gather x2 -> x1, waiting for transfers between devices: 173 us -> 0.01 us  [body(): all_grads = lax.all_gather(shard, 'lat', axis=0, tiled=True)]
    reduce_scatter x1 -> x0, waiting for transfers between devices: 110 us -> none  [body(): lax.psum_scatter(returned_part.astype(jnp.bfloat16), 'lat', scatter_dimen...]
    pallas_call x0 -> x6, Pallas kernels: none -> 105 us  [the longest x2 46.1 us: expert_side(): pl.pallas_call(expert_kernel, out_shape=(part,) * 4 + (jax.ShapeDtypeStru...]
    ppermute x8 -> x54, waiting for transfers between devices: 33 us -> 119 us  [the longest x36 78.9 us: swapped(): lax.ppermute(block, axis, [(i, i ^ direction) for i in range(lax.axis_siz...]
    dot_general x9 -> x4, matrix products: 70.6 us -> 6.66 us  [the longest x1 5.92 us: attention_forward(): jnp.dot(normed.reshape(-1, features), weight_in, preferred_element_type=j...]
    ppermute x8 -> x54, starting transfers between devices: 14.1 us -> 62.6 us  [the longest x36 34 us: swapped(): lax.ppermute(block, axis, [(i, i ^ direction) for i in range(lax.axis_siz...]
    all_to_all x2 -> x0, blocking collectives: 41.6 us -> none  [the longest x1 23.1 us: body(): lax.all_to_all(send_in, 'lon', split_axis=1, concat_axis=1, tiled=True)]
    unnamed x37 -> x95, local copies, waits for them, and re-layouts: 3.99 us -> 34.8 us
  transfers between devices with their start and end apart: 12 -> 55, of which waited for: 10 -> 30; matrix products, arithmetic and copies ran while one was open for 8% -> 27% of each run, Pallas kernels for 0% -> 22%
where the time goes in v1:
time: 482 us; the launch traced here: 475 us
  waiting for transfers between devices  119 us (25%)
  Pallas kernels  105 us (22%)
  local copies, waits for them, and re-layouts  97.4 us (20%)
  starting transfers between devices  62.7 us (13%)
  matrix products  40.6 us (8%)
  other arithmetic  35.4 us (7%)
  between operations  15.7 us (3%)
    ppermute x36, waiting for transfers between devices, swapped(): lax.ppermute(block, axis, [(i, i ^ direction) for i in range(lax.axis_siz...  78.9 us
    pallas_call x2, Pallas kernels, expert_side(): pl.pallas_call(expert_kernel, out_shape=(part,) * 4 + (jax.ShapeDtypeStru...  46.1 us
    pallas_call x2, Pallas kernels, weight_side(): pl.pallas_call(weight_kernel, out_shape=(jax.ShapeDtypeStruct((EPG, featu...  35.5 us
    unnamed x95, local copies, waits for them, and re-layouts  34.8 us
    ppermute x36, starting transfers between devices, swapped(): lax.ppermute(block, axis, [(i, i ^ direction) for i in range(lax.axis_siz...  34 us
    ppermute x9, waiting for transfers between devices, turned(): lax.ppermute(block, 'lon', [(i, (i + distance) % devices) for i in range(...  25.4 us
    pallas_call x2, Pallas kernels, grad_side(): pl.pallas_call(grad_kernel, out_shape=(jax.ShapeDtypeStruct((BUFFER, feat...  23 us
    ppermute x9, starting transfers between devices, moved(): return lax.ppermute(block, ('lon', 'lat'), route)  19.5 us
  transfers between devices with their start and end apart: 55, of which 30 were waited for; matrix products, arithmetic and copies ran while one was open for 27% of the time, Pallas kernels for 22%

profile of v1, /device:TPU:1, one launch (start us, length us, event | category | flops | bytes accessed | tf_op | source)
XLA Modules:
  0.0 475.3 jit_solution(349161116657020723)
XLA Ops:
  13.8 7.0 %collective-permute-start.3 = (bf16[9,16,1024]{2,1,0:T(8,128)(2,1)}, bf16[9,16,1024]{2,1,0:T(8,128)(2,1)}, u32[]{:S(2)}, u32[]{:S(2)}) collective-permute-start(bf16[9,16,1024]{2,1,0:T(8,128)(2,1)} %reshape.510), channel_id=1, source_target_pairs={{0,15},{1,0},{2,1},{3,2},{4,3},{5,4},{6,5},{7,6},{8,7},{9,8},{10,9... | collective-permute-start | bytes 884744 | tf_op jit(solution)/shard_map/ppermute | solution.py:57
  29.7 4.6 collective-permute-done.5
  44.3 4.5 collective-permute-done.7
  50.8 6.5 %concatenate.83 = bf16[272,1024]{1,0:T(8,128)(2,1)} concatenate(bf16[64,1024]{1,0:T(8,128)(2,1)S(1)} %dynamic-slice_bitcast_fusion.3, bf16[64,1024]{1,0:T(8,128)(2,1)S(1)} %slice.259, bf16[64,1024]{1,0:T(8,128)(2,1)} %slice.260, bf16[64,1024]{1,0:T(8,128)(2,1)} %slice.261, bf16[1,1024]{1,0:T(2,128)(2,1)S(1)} %dynamic-slice_bitcast_fusion.8, bf16[1,1024]{1,0:T(2,128)(2,1)S(1)} %slice.262, ...), dimensions={0} | concatenate | bytes 1114112 | tf_op jit(solution)/shard_map/concatenate | solution.py:536
  63.4 5.9 %convolution_convert_fusion = bf16[256,3072]{1,0:T(8,128)(2,1)} fusion(bf16[256,1024]{1,0:T(8,128)(2,1)S(1)} %bitcast.161, bf16[1024,3072]{1,0:T(8,128)(2,1)} %param.14), kind=kOutput, calls=%fused_computation.6 | convolution fusion | flops 1611399168 | bytes 8388608 | tf_op jit(solution)/shard_map/dot_general | solution.py:395
  69.3 4.9 %reshape.514 = bf16[4,64,3,16,64]{4,3,2,1,0:T(8,128)(2,1)} reshape(bf16[256,3072]{1,0:T(8,128)(2,1)} %convolution_convert_fusion) | data formatting | bytes 3145728 | tf_op jit(solution)/shard_map/reshape | solution.py:396
  74.2 3.8 fusion.121
  80.7 4.7 fusion.127
  85.4 3.3 fusion.23
  106.2 3.3 collective-permute-done.16
  119.4 5.3 %collective-permute-done.13 = bf16[64,1024]{1,0:T(8,128)(2,1)S(1)} collective-permute-done((bf16[64,1024]{1,0:T(8,128)(2,1)S(1)}, bf16[64,1024]{1,0:T(8,128)(2,1)S(1)}, u32[]{:S(2)}, u32[]{:S(2)}) %collective-permute-start.13) | collective-permute-done | bytes 131104 | tf_op jit(solution)/shard_map/ppermute | solution.py:42
  132.7 4.0 collective-permute-done.14
  136.7 3.2 collective-permute-start.15
  142.1 5.7 %collective-permute-done.11 = bf16[256,1024]{1,0:T(8,128)(2,1)S(1)} collective-permute-done((bf16[256,1024]{1,0:T(8,128)(2,1)S(1)}, bf16[256,1024]{1,0:T(8,128)(2,1)S(1)}, u32[]{:S(2)}, u32[]{:S(2)}) %collective-permute-start.11) | collective-permute-done | bytes 524320 | tf_op jit(solution)/shard_map/ppermute | solution.py:42
  161.2 11.3 %shard_map.132 = (bf16[5120,1024]{1,0:T(8,128)(2,1)}, f32[5120,256]{1,0:T(8,128)S(1)}) custom-call(s32[8,24]{1,0:T(8,128)S(1)} %broadcast_add_fusion.place_ref, s32[21]{0:T(128)S(1)} %pad_add_fusion.1.plan_ref, s32[32]{0:T(128)S(1)} %reshape.520.offset_ref, bf16[4352,1024]{1,0:T(8,128)(2,1)} %all-gather.2.cloned.1.call-done.rows_ref, ...), custom_call_target="tpu_custom_call" | custom-call | flops 6000000000 | bytes 25165824 | tf_op jit(solution)/shard_map/pallas_call | solution.py:163
  178.6 3.7 collective-permute-done.27.rows1_ref
  182.3 22.6 %shard_map.133 = (bf16[512,1024]{1,0:T(8,128)(2,1)S(1)}, bf16[512,1024]{1,0:T(8,128)(2,1)}, bf16[512,1024]{1,0:T(8,128)(2,1)}, bf16[512,1024]{1,0:T(8,128)(2,1)}...) custom-call(s32[8,24]{1,0:T(8,128)S(1)} %broadcast_add_fusion.place_ref, ...), custom_call_target="tpu_custom_call" | custom-call | flops 10000000000 | bytes 33554432 | tf_op jit(solution)/shard_map/pallas_call | solution.py:280
  204.9 3.1 collective-permute-start.44
  212.8 11.7 %shard_map.130 = (bf16[5120,1024]{1,0:T(8,128)(2,1)}, f32[5120,256]{1,0:T(8,128)S(1)}) custom-call(s32[8,24]{1,0:T(8,128)S(1)} %broadcast_add_fusion.1.place_ref, s32[21]{0:T(128)S(1)} %pad_add_fusion.plan_ref, s32[32]{0:T(128)S(1)} %reshape.518.offset_ref, bf16[4352,1024]{1,0:T(8,128)(2,1)} %all-gather.2.cloned.1.call-done.rows_ref, ...), custom_call_target="tpu_custom_call" | custom-call | flops 6000000000 | bytes 25165824 | tf_op jit(solution)/shard_map/pallas_call | solution.py:163
  226.8 23.5 %shard_map.131 = (bf16[512,1024]{1,0:T(8,128)(2,1)S(1)}, bf16[512,1024]{1,0:T(8,128)(2,1)}, bf16[512,1024]{1,0:T(8,128)(2,1)}, bf16[512,1024]{1,0:T(8,128)(2,1)}...) custom-call(s32[8,24]{1,0:T(8,128)S(1)} %broadcast_add_fusion.1.place_ref, ...), custom_call_target="tpu_custom_call" | custom-call | flops 10000000000 | bytes 33554432 | tf_op jit(solution)/shard_map/pallas_call | solution.py:280
  253.8 16.1 %shard_map.134 = (f32[8,1024,256]{2,1,0:T(8,128)S(1)}, f32[8,256,1024]{2,1,0:T(8,128)S(1)}) custom-call(s32[21]{0:T(128)S(1)} %pad_add_fusion.plan_ref, bf16[5120,1024]{1,0:T(8,128)(2,1)} %get-tuple-element.39.rows_ref, bf16[5120,256]{1,0:T(8,128)(2,1)S(1)} %copy-done.8, bf16[5120,256]{1,0:T(8,128)(2,1)S(1)} %copy-done.7, ...), custom_call_target="tpu_custom_call" | custom-call | flops 4000000000 | bytes 33554432 | tf_op jit(solution)/shard_map/pallas_call | solution.py:341
  269.9 3.2 copy-done.3
  273.2 3.3 copy-done.4
  276.5 19.4 %shard_map.135 = (f32[8,1024,256]{2,1,0:T(8,128)S(1)}, f32[8,256,1024]{2,1,0:T(8,128)S(1)}) custom-call(s32[21]{0:T(128)S(1)} %pad_add_fusion.1.plan_ref, bf16[5120,1024]{1,0:T(8,128)(2,1)} %get-tuple-element.35.rows_ref, bf16[5120,256]{1,0:T(8,128)(2,1)S(1)} %copy-done.6, bf16[5120,256]{1,0:T(8,128)(2,1)S(1)} %copy-done.5, ...), custom_call_target="tpu_custom_call" | custom-call | flops 4000000000 | bytes 33554432 | tf_op jit(solution)/shard_map/pallas_call | solution.py:341
  296.0 3.0 slice.247
  306.3 6.1 %collective-permute-start.2 = (bf16[4,16,1024]{2,1,0:T(8,128)(2,1)S(1)}, bf16[4,16,1024]{2,1,0:T(8,128)(2,1)S(1)}, u32[]{:S(2)}, u32[]{:S(2)}) collective-permute-start(bf16[4,16,1024]{2,1,0:T(8,128)(2,1)S(1)} %copy-done.30), channel_id=1, source_target_pairs={{0,127},{1,112},{2,113},{3,114},{4,115},{5,116},{6,117},{7,118},{8... | collective-permute-start | bytes 393224 | tf_op jit(solution)/shard_map/ppermute | solution.py:57
  317.8 10.2 %collective-permute-done.45 = bf16[256,1024]{1,0:T(8,128)(2,1)S(1)} collective-permute-done((bf16[256,1024]{1,0:T(8,128)(2,1)S(1)}, bf16[256,1024]{1,0:T(8,128)(2,1)S(1)}, u32[]{:S(2)}, u32[]{:S(2)}) %collective-permute-start.45) | collective-permute-done | bytes 524320 | tf_op jit(solution)/shard_map/ppermute | solution.py:42
  330.2 11.7 %collective-permute-done.35 = bf16[256,1024]{1,0:T(8,128)(2,1)S(1)} collective-permute-done((bf16[256,1024]{1,0:T(8,128)(2,1)S(1)}, bf16[256,1024]{1,0:T(8,128)(2,1)S(1)}, u32[]{:S(2)}, u32[]{:S(2)}) %collective-permute-start.35) | collective-permute-done | bytes 524320 | tf_op jit(solution)/shard_map/ppermute | solution.py:42
  344.8 3.3 collective-permute-done.46
  351.2 3.3 collective-permute-done.36
  354.6 3.7 collective-permute-start.53
  359.0 4.5 collective-permute-done.47
  363.5 5.0 %collective-permute-done.42 = bf16[64,1024]{1,0:T(8,128)(2,1)S(1)} collective-permute-done((bf16[64,1024]{1,0:T(8,128)(2,1)S(1)}, bf16[64,1024]{1,0:T(8,128)(2,1)S(1)}, u32[]{:S(2)}, u32[]{:S(2)}) %collective-permute-start.42) | collective-permute-done | bytes 131104 | tf_op jit(solution)/shard_map/ppermute | solution.py:42
  368.5 3.8 collective-permute-done.37
  372.3 4.1 collective-permute-done.33
  376.6 3.9 collective-permute-done.38
  382.0 3.8 collective-permute-done.43
  385.9 5.0 %collective-permute-done.48 = bf16[64,1024]{1,0:T(8,128)(2,1)S(1)} collective-permute-done((bf16[64,1024]{1,0:T(8,128)(2,1)S(1)}, bf16[64,1024]{1,0:T(8,128)(2,1)S(1)}, u32[]{:S(2)}, u32[]{:S(2)}) %collective-permute-start.48) | collective-permute-done | bytes 131104 | tf_op jit(solution)/shard_map/ppermute | solution.py:47
  390.9 9.3 %collective-permute-start.52 = (f32[4,1024,256]{2,1,0:T(8,128)}, f32[4,1024,256]{2,1,0:T(8,128)}, u32[]{:S(2)}, u32[]{:S(2)}) collective-permute-start(f32[4,1024,256]{2,1,0:T(8,128)} %slice.245), channel_id=1, source_target_pairs={{0,16},{16,0},{32,48},{48,32},{64,80},{80,64},{96,112},{112,96},{1... | collective-permute-start | bytes 12582920 | tf_op jit(solution)/shard_map/ppermute | solution.py:42
  407.8 3.5 fusion.56
  411.3 5.6 %fusion.28 = bf16[4,64,1,16,64]{1,4,3,0,2:T(8,128)(2,1)} fusion(f32[4,16,64,64]{2,3,1,0:T(8,128)} %fusion.56, bf16[4,64,1,16,64]{4,3,2,1,0:T(8,128)(2,1)S(1)} %copy-done.25, f32[4,16,64,64]{2,3,1,0:T(8,128)} %get-tuple-element.96, f32[4,16,64]{2,1,0:T(8,128)S(1)} %copy-done.37), kind=kOutput, calls=%fused_computation.36 | convolution fusion | flops 35655744 | bytes 3162112 | tf_op jit(solution)/shard_map/whqk,wkhe->wqhe/dot_general | solution.py:433
  416.9 5.9 %fusion.25 = bf16[4,64,1,16,64]{1,4,3,0,2:T(8,128)(2,1)} fusion(f32[4,16,64,64]{2,3,1,0:T(8,128)} %fusion.56, bf16[4,64,1,16,64]{4,3,2,1,0:T(8,128)(2,1)} %get-tuple-element.67, f32[4,16,64,64]{2,3,1,0:T(8,128)} %get-tuple-element.96, f32[4,16,64]{2,1,0:T(8,128)S(1)} %copy-done.37), kind=kOutput, calls=%fused_computation.35 | convolution fusion | flops 35655744 | bytes 3162112 | tf_op jit(solution)/shard_map/whqk,wqhe->wkhe/dot_general | solution.py:434
  427.7 5.3 %copy.126 = bf16[4,64,3,16,64]{4,3,2,1,0:T(8,128)(2,1)} copy(bf16[4,64,3,16,64]{1,4,3,0,2:T(8,128)(2,1)} %pad_maximum_fusion) | data formatting | bytes 3145728 | tf_op jit(solution)/shard_map/stack | solution.py:436
  433.0 5.0 %convert_element_type.429 = bf16[4,64,3072]{2,1,0:T(8,128)(2,1)} reshape(bf16[4,64,3,16,64]{4,3,2,1,0:T(8,128)(2,1)} %copy.126) | data formatting | bytes 3145728 | tf_op jit(solution)/shard_map/convert_element_type | solution.py:437
  438.0 5.2 %fusion.55 = (f32[4,64]{1,0:T(4,128)S(1)}, f32[4,64,1024]{2,1,0:T(8,128)S(1)}) fusion(bf16[9,64,1024]{2,1,0:T(8,128)(2,1)S(1)} %copy-done.16, f32[1024]{0:T(1024)S(1)} %copy-done.35, bf16[4,64,3072]{2,1,0:T(8,128)(2,1)} %convert_element_type.429, bf16[1024,3072]{1,0:T(8,128)(2,1)} %param.14), kind=kOutput, calls=%fused_computation.68 | convolution fusion | flops 1611661056 | bytes 9442304 | tf_op jit(solution)/shard_map/dot_general | solution.py:440
  444.0 9.9 %collective-permute-done.49 = bf16[4,16,1024]{2,1,0:T(8,128)(2,1)S(1)} collective-permute-done((bf16[4,16,1024]{2,1,0:T(8,128)(2,1)S(1)}, bf16[4,16,1024]{2,1,0:T(8,128)(2,1)S(1)}, u32[]{:S(2)}, u32[]{:S(2)}) %collective-permute-start.49) | collective-permute-done | bytes 131104 | tf_op jit(solution)/shard_map/ppermute | solution.py:57
  455.1 6.8 %slice_add_fusion = f32[4,256,1024]{2,1,0:T(8,128)} fusion(f32[4,256,1024]{2,1,0:T(8,128)} %collective-permute-done.53, f32[8,256,1024]{2,1,0:T(8,128)} %copy-done.2), kind=kLoop, calls=%fused_computation.4 | loop fusion | flops 1048576 | bytes 12582912 | tf_op jit(solution)/shard_map/add | solution.py:579
  461.9 6.0 %slice_add_fusion.1 = f32[4,1024,256]{2,1,0:T(8,128)} fusion(f32[4,1024,256]{2,1,0:T(8,128)} %collective-permute-done.52, f32[8,1024,256]{2,1,0:T(8,128)} %copy-done.1), kind=kLoop, calls=%fused_computation.5 | loop fusion | flops 1048576 | bytes 12582912 | tf_op jit(solution)/shard_map/add | solution.py:578
  (325 shorter events, 141.1 us)
Async XLA Ops:
  7.2 147.3 %all-gather.2.cloned.1.call-start = ((), (), s32[]{:S(2)}) async-start(), calls=%async_computation | async-start | bytes 9469952 | tf_op jit(solution)/shard_map/all_gather | solution.py:542
  13.8 13.7 %collective-permute-start.3 = (bf16[9,16,1024]{2,1,0:T(8,128)(2,1)}, bf16[9,16,1024]{2,1,0:T(8,128)(2,1)}, u32[]{:S(2)}, u32[]{:S(2)}) collective-permute-start(bf16[9,16,1024]{2,1,0:T(8,128)(2,1)} %reshape.510), channel_id=1, source_target_pairs={{0,15},{1,0},{2,1},{3,2},{4,3},{5,4},{6,5},{7,6},{8,7},{9,8},{10,9... | collective-permute-start | bytes 884744 | tf_op jit(solution)/shard_map/ppermute | solution.py:57
  21.6 7.1 %collective-permute-start.4 = (bf16[9,16,1024]{2,1,0:T(8,128)(2,1)}, bf16[9,16,1024]{2,1,0:T(8,128)(2,1)}, u32[]{:S(2)}, u32[]{:S(2)}) collective-permute-start(bf16[9,16,1024]{2,1,0:T(8,128)(2,1)} %reshape.511), channel_id=1, source_target_pairs={{0,112},{1,113},{2,114},{3,115},{4,116},{5,117},{6,118},{7,119},{8... | collective-permute-start | bytes 884744 | tf_op jit(solution)/shard_map/ppermute | solution.py:57
  23.4 10.9 %collective-permute-start.5 = (bf16[9,16,1024]{2,1,0:T(8,128)(2,1)}, bf16[9,16,1024]{2,1,0:T(8,128)(2,1)}, u32[]{:S(2)}, u32[]{:S(2)}) collective-permute-start(bf16[9,16,1024]{2,1,0:T(8,128)(2,1)} %reshape.512), channel_id=1, source_target_pairs={{0,127},{1,112},{2,113},{3,114},{4,115},{5,116},{6,117},{7,118},{8... | collective-permute-start | bytes 884744 | tf_op jit(solution)/shard_map/ppermute | solution.py:57
  37.5 6.8 %collective-permute-start.6 = (bf16[80,1024]{1,0:T(8,128)(2,1)S(1)}, bf16[80,1024]{1,0:T(8,128)(2,1)S(1)}, u32[]{:S(2)}, u32[]{:S(2)}) collective-permute-start(bf16[80,1024]{1,0:T(8,128)(2,1)S(1)} %get-tuple-element.74), channel_id=1, source_target_pairs={{0,32},{16,48},{32,64},{48,80},{64,96},{80,112},{96,0},{112,16},{1... | collective-permute-start | bytes 491528 | tf_op jit(solution)/shard_map/ppermute | solution.py:47
  38.8 10.1 %collective-permute-start.7 = (bf16[80,1024]{1,0:T(8,128)(2,1)S(1)}, bf16[80,1024]{1,0:T(8,128)(2,1)S(1)}, u32[]{:S(2)}, u32[]{:S(2)}) collective-permute-start(bf16[80,1024]{1,0:T(8,128)(2,1)S(1)} %get-tuple-element.73), channel_id=1, source_target_pairs={{0,64},{16,80},{32,96},{48,112},{64,0},{80,16},{96,32},{112,48},{1... | collective-permute-start | bytes 491528 | tf_op jit(solution)/shard_map/ppermute | solution.py:47
  41.2 8.3 %collective-permute-start.8 = (bf16[80,1024]{1,0:T(8,128)(2,1)S(1)}, bf16[80,1024]{1,0:T(8,128)(2,1)S(1)}, u32[]{:S(2)}, u32[]{:S(2)}) collective-permute-start(bf16[80,1024]{1,0:T(8,128)(2,1)S(1)} %get-tuple-element.72), channel_id=1, source_target_pairs={{0,96},{16,112},{32,0},{48,16},{64,32},{80,48},{96,64},{112,80},{1... | collective-permute-start | bytes 491528 | tf_op jit(solution)/shard_map/ppermute | solution.py:47
  57.3 101.2 %collective-permute-start.25 = (bf16[4,256,1024]{2,1,0:T(8,128)(2,1)}, bf16[4,256,1024]{2,1,0:T(8,128)(2,1)}, u32[]{:S(2)}, u32[]{:S(2)}) collective-permute-start(bf16[4,256,1024]{2,1,0:T(8,128)(2,1)} %own_ref.6), channel_id=1, source_target_pairs={{0,16},{16,0},{32,48},{48,32},{64,80},{80,64},{96,112},{112,96},{1... | collective-permute-start | bytes 6291464 | tf_op jit(solution)/shard_map/ppermute | solution.py:42
  97.0 8.3 %collective-permute-start.9 = (bf16[64,1024]{1,0:T(8,128)(2,1)S(1)}, bf16[64,1024]{1,0:T(8,128)(2,1)S(1)}, u32[]{:S(2)}, u32[]{:S(2)}) collective-permute-start(bf16[64,1024]{1,0:T(8,128)(2,1)S(1)} %get-tuple-element.82), channel_id=1, source_target_pairs={{0,1},{1,0},{2,3},{3,2},{4,5},{5,4},{6,7},{7,6},{8,9},{9,8},{10,11... | collective-permute-start | bytes 393224 | tf_op jit(solution)/shard_map/ppermute | solution.py:42
  97.1 8.3 %collective-permute-start.20 = (bf16[64,1024]{1,0:T(8,128)(2,1)S(1)}, bf16[64,1024]{1,0:T(8,128)(2,1)S(1)}, u32[]{:S(2)}, u32[]{:S(2)}) collective-permute-start(bf16[64,1024]{1,0:T(8,128)(2,1)S(1)} %get-tuple-element.79), channel_id=1, source_target_pairs={{0,96},{16,112},{32,0},{48,16},{64,32},{80,48},{96,64},{112,80},{1... | collective-permute-start | bytes 393224 | tf_op jit(solution)/shard_map/ppermute | solution.py:47
  103.2 6.2 %collective-permute-start.16 = (bf16[64,1024]{1,0:T(8,128)(2,1)S(1)}, bf16[64,1024]{1,0:T(8,128)(2,1)S(1)}, u32[]{:S(2)}, u32[]{:S(2)}) collective-permute-start(bf16[64,1024]{1,0:T(8,128)(2,1)S(1)} %get-tuple-element.80), channel_id=1, source_target_pairs={{0,64},{16,80},{32,96},{48,112},{64,0},{80,16},{96,32},{112,48},{1... | collective-permute-start | bytes 393224 | tf_op jit(solution)/shard_map/ppermute | solution.py:47
  104.1 9.0 %collective-permute-start.12 = (bf16[64,1024]{1,0:T(8,128)(2,1)S(1)}, bf16[64,1024]{1,0:T(8,128)(2,1)S(1)}, u32[]{:S(2)}, u32[]{:S(2)}) collective-permute-start(bf16[64,1024]{1,0:T(8,128)(2,1)S(1)} %get-tuple-element.81), channel_id=1, source_target_pairs={{0,32},{16,48},{32,64},{48,80},{64,96},{80,112},{96,0},{112,16},{1... | collective-permute-start | bytes 393224 | tf_op jit(solution)/shard_map/ppermute | solution.py:47
  105.3 21.4 %collective-permute-start.10 = (bf16[128,1024]{1,0:T(8,128)(2,1)S(1)}, bf16[128,1024]{1,0:T(8,128)(2,1)S(1)}, u32[]{:S(2)}, u32[]{:S(2)}) collective-permute-start(bf16[128,1024]{1,0:T(8,128)(2,1)S(1)} %pad_maximum_fusion.7), channel_id=1, source_target_pairs={{0,4},{1,5},{2,6},{3,7},{4,0},{5,1},{6,2},{7,3},{8,12},{9,13},{10,... | collective-permute-start | bytes 786440 | tf_op jit(solution)/shard_map/ppermute | solution.py:42
  105.4 9.3 %collective-permute-start.21 = (bf16[64,1024]{1,0:T(8,128)(2,1)S(1)}, bf16[64,1024]{1,0:T(8,128)(2,1)S(1)}, u32[]{:S(2)}, u32[]{:S(2)}) collective-permute-start(bf16[64,1024]{1,0:T(8,128)(2,1)S(1)} %collective-permute-done.20), channel_id=1, source_target_pairs={{0,12},{1,13},{2,14},{3,15},{4,8},{5,9},{6,10},{7,11},{8,4},{9,5},... | collective-permute-start | bytes 393224 | tf_op jit(solution)/shard_map/ppermute | solution.py:42
  109.5 8.8 %collective-permute-start.17 = (bf16[64,1024]{1,0:T(8,128)(2,1)S(1)}, bf16[64,1024]{1,0:T(8,128)(2,1)S(1)}, u32[]{:S(2)}, u32[]{:S(2)}) collective-permute-start(bf16[64,1024]{1,0:T(8,128)(2,1)S(1)} %collective-permute-done.16), channel_id=1, source_target_pairs={{0,3},{1,2},{2,1},{3,0},{4,7},{5,6},{6,5},{7,4},{8,11},{9,10},{10,... | collective-permute-start | bytes 393224 | tf_op jit(solution)/shard_map/ppermute | solution.py:42
  113.1 11.6 %collective-permute-start.13 = (bf16[64,1024]{1,0:T(8,128)(2,1)S(1)}, bf16[64,1024]{1,0:T(8,128)(2,1)S(1)}, u32[]{:S(2)}, u32[]{:S(2)}) collective-permute-start(bf16[64,1024]{1,0:T(8,128)(2,1)S(1)} %collective-permute-done.12), channel_id=1, source_target_pairs={{0,4},{1,5},{2,6},{3,7},{4,0},{5,1},{6,2},{7,3},{8,12},{9,13},{10,... | collective-permute-start | bytes 393224 | tf_op jit(solution)/shard_map/ppermute | solution.py:42
  114.8 14.8 %collective-permute-start.22 = (bf16[128,1024]{1,0:T(8,128)(2,1)S(1)}, bf16[128,1024]{1,0:T(8,128)(2,1)S(1)}, u32[]{:S(2)}, u32[]{:S(2)}) collective-permute-start(bf16[128,1024]{1,0:T(8,128)(2,1)S(1)} %pad_maximum_fusion.10), channel_id=1, source_target_pairs={{0,1},{1,0},{2,3},{3,2},{4,5},{5,4},{6,7},{7,6},{8,9},{9,8},{10,11... | collective-permute-start | bytes 786440 | tf_op jit(solution)/shard_map/ppermute | solution.py:42
  118.3 14.2 %collective-permute-start.18 = (bf16[128,1024]{1,0:T(8,128)(2,1)S(1)}, bf16[128,1024]{1,0:T(8,128)(2,1)S(1)}, u32[]{:S(2)}, u32[]{:S(2)}) collective-permute-start(bf16[128,1024]{1,0:T(8,128)(2,1)S(1)} %pad_maximum_fusion.9), channel_id=1, source_target_pairs={{0,12},{1,13},{2,14},{3,15},{4,8},{5,9},{6,10},{7,11},{8,4},{9,5},... | collective-permute-start | bytes 786440 | tf_op jit(solution)/shard_map/ppermute | solution.py:42
  124.7 12.0 %collective-permute-start.14 = (bf16[128,1024]{1,0:T(8,128)(2,1)S(1)}, bf16[128,1024]{1,0:T(8,128)(2,1)S(1)}, u32[]{:S(2)}, u32[]{:S(2)}) collective-permute-start(bf16[128,1024]{1,0:T(8,128)(2,1)S(1)} %pad_maximum_fusion.8), channel_id=1, source_target_pairs={{0,3},{1,2},{2,1},{3,0},{4,7},{5,6},{6,5},{7,4},{8,11},{9,10},{10,... | collective-permute-start | bytes 786440 | tf_op jit(solution)/shard_map/ppermute | solution.py:42
  126.8 21.0 %collective-permute-start.11 = (bf16[256,1024]{1,0:T(8,128)(2,1)S(1)}, bf16[256,1024]{1,0:T(8,128)(2,1)S(1)}, u32[]{:S(2)}, u32[]{:S(2)}) collective-permute-start(bf16[256,1024]{1,0:T(8,128)(2,1)S(1)} %pad_maximum_fusion.3), channel_id=1, source_target_pairs={{0,3},{1,2},{2,1},{3,0},{4,7},{5,6},{6,5},{7,4},{8,11},{9,10},{10,... | collective-permute-start | bytes 1572872 | tf_op jit(solution)/shard_map/ppermute | solution.py:42
  129.6 19.4 %collective-permute-start.23 = (bf16[256,1024]{1,0:T(8,128)(2,1)S(1)}, bf16[256,1024]{1,0:T(8,128)(2,1)S(1)}, u32[]{:S(2)}, u32[]{:S(2)}) collective-permute-start(bf16[256,1024]{1,0:T(8,128)(2,1)S(1)} %pad_maximum_fusion.6), channel_id=1, source_target_pairs={{0,4},{1,5},{2,6},{3,7},{4,0},{5,1},{6,2},{7,3},{8,12},{9,13},{10,... | collective-permute-start | bytes 1572872 | tf_op jit(solution)/shard_map/ppermute | solution.py:42
  132.6 20.0 %collective-permute-start.19 = (bf16[256,1024]{1,0:T(8,128)(2,1)S(1)}, bf16[256,1024]{1,0:T(8,128)(2,1)S(1)}, u32[]{:S(2)}, u32[]{:S(2)}) collective-permute-start(bf16[256,1024]{1,0:T(8,128)(2,1)S(1)} %pad_maximum_fusion.5), channel_id=1, source_target_pairs={{0,1},{1,0},{2,3},{3,2},{4,5},{5,4},{6,7},{7,6},{8,9},{9,8},{10,11... | collective-permute-start | bytes 1572872 | tf_op jit(solution)/shard_map/ppermute | solution.py:42
  136.7 16.9 %collective-permute-start.15 = (bf16[256,1024]{1,0:T(8,128)(2,1)S(1)}, bf16[256,1024]{1,0:T(8,128)(2,1)S(1)}, u32[]{:S(2)}, u32[]{:S(2)}) collective-permute-start(bf16[256,1024]{1,0:T(8,128)(2,1)S(1)} %pad_maximum_fusion.4), channel_id=1, source_target_pairs={{0,12},{1,13},{2,14},{3,15},{4,8},{5,9},{6,10},{7,11},{8,4},{9,5},... | collective-permute-start | bytes 1572872 | tf_op jit(solution)/shard_map/ppermute | solution.py:42
  147.8 27.1 %collective-permute-start.24 = (bf16[4,1024,256]{2,1,0:T(8,128)(2,1)}, bf16[4,1024,256]{2,1,0:T(8,128)(2,1)}, u32[]{:S(2)}, u32[]{:S(2)}) collective-permute-start(bf16[4,1024,256]{2,1,0:T(8,128)(2,1)} %own_ref.7), channel_id=1, source_target_pairs={{0,16},{16,0},{32,48},{48,32},{64,80},{80,64},{96,112},{112,96},{1... | collective-permute-start | bytes 6291464 | tf_op jit(solution)/shard_map/ppermute | solution.py:42
  148.9 28.8 %collective-permute-start.26 = (bf16[512,1024]{1,0:T(8,128)(2,1)S(1)}, bf16[512,1024]{1,0:T(8,128)(2,1)}, u32[]{:S(2)}, u32[]{:S(2)}) collective-permute-start(bf16[512,1024]{1,0:T(8,128)(2,1)S(1)} %pad_maximum_fusion.2.rows0_ref), channel_id=1, source_target_pairs={{0,12},{1,13},{2,14},{3,15},{4,8},{5,9},{6,10},{7,11},{8,4},{9,5},... | collective-permute-start | bytes 3145736 | tf_op jit(solution)/shard_map/ppermute | solution.py:42
  152.6 26.0 %collective-permute-start.29 = (bf16[512,1024]{1,0:T(8,128)(2,1)}, bf16[512,1024]{1,0:T(8,128)(2,1)}, u32[]{:S(2)}, u32[]{:S(2)}) collective-permute-start(bf16[512,1024]{1,0:T(8,128)(2,1)} %constant_dynamic-update-slice_fusion.12.rows3_ref), channel_id=1, source_target_pairs={{0,3},{1,2},{2,1},{3,0},{4,7},{5,6},{6,5},{7,4},{8,11},{9,10},{10,... | collective-permute-start | bytes 3145736 | tf_op jit(solution)/shard_map/ppermute | solution.py:42
  153.6 24.9 %collective-permute-start.28 = (bf16[512,1024]{1,0:T(8,128)(2,1)}, bf16[512,1024]{1,0:T(8,128)(2,1)}, u32[]{:S(2)}, u32[]{:S(2)}) collective-permute-start(bf16[512,1024]{1,0:T(8,128)(2,1)} %constant_dynamic-update-slice_fusion.8.rows2_ref), channel_id=1, source_target_pairs={{0,4},{1,5},{2,6},{3,7},{4,0},{5,1},{6,2},{7,3},{8,12},{9,13},{10,... | collective-permute-start | bytes 3145736 | tf_op jit(solution)/shard_map/ppermute | solution.py:42
  158.5 23.8 %collective-permute-start.27 = (bf16[512,1024]{1,0:T(8,128)(2,1)}, bf16[512,1024]{1,0:T(8,128)(2,1)}, u32[]{:S(2)}, u32[]{:S(2)}) collective-permute-start(bf16[512,1024]{1,0:T(8,128)(2,1)} %constant_dynamic-update-slice_fusion.4.rows1_ref), channel_id=1, source_target_pairs={{0,1},{1,0},{2,3},{3,2},{4,5},{5,4},{6,7},{7,6},{8,9},{9,8},{10,11... | collective-permute-start | bytes 3145736 | tf_op jit(solution)/shard_map/ppermute | solution.py:42
  174.9 225.6 %collective-permute-start = (bf16[4,16,1024]{2,1,0:T(8,128)(2,1)}, bf16[4,16,1024]{2,1,0:T(8,128)(2,1)}, u32[]{:S(2)}, u32[]{:S(2)}) collective-permute-start(bf16[4,16,1024]{2,1,0:T(8,128)(2,1)} %reshape.506), channel_id=1, source_target_pairs={{0,15},{1,0},{2,1},{3,2},{4,3},{5,4},{6,5},{7,6},{8,7},{9,8},{10,9... | collective-permute-start | bytes 393224 | tf_op jit(solution)/shard_map/ppermute | solution.py:57
  204.9 99.6 %collective-permute-start.44 = (bf16[512,1024]{1,0:T(8,128)(2,1)}, bf16[512,1024]{1,0:T(8,128)(2,1)}, u32[]{:S(2)}, u32[]{:S(2)}) collective-permute-start(bf16[512,1024]{1,0:T(8,128)(2,1)} %get-tuple-element.34), channel_id=1, source_target_pairs={{0,3},{1,2},{2,1},{3,0},{4,7},{5,6},{6,5},{7,4},{8,11},{9,10},{10,... | collective-permute-start | bytes 3145736 | tf_op jit(solution)/shard_map/ppermute | solution.py:42
  208.0 98.3 %collective-permute-start.39 = (bf16[512,1024]{1,0:T(8,128)(2,1)}, bf16[512,1024]{1,0:T(8,128)(2,1)}, u32[]{:S(2)}, u32[]{:S(2)}) collective-permute-start(bf16[512,1024]{1,0:T(8,128)(2,1)} %get-tuple-element.32), channel_id=1, source_target_pairs={{0,4},{1,5},{2,6},{3,7},{4,0},{5,1},{6,2},{7,3},{8,12},{9,13},{10,... | collective-permute-start | bytes 3145736 | tf_op jit(solution)/shard_map/ppermute | solution.py:42
  210.4 103.9 %collective-permute-start.34 = (bf16[512,1024]{1,0:T(8,128)(2,1)}, bf16[512,1024]{1,0:T(8,128)(2,1)}, u32[]{:S(2)}, u32[]{:S(2)}) collective-permute-start(bf16[512,1024]{1,0:T(8,128)(2,1)} %get-tuple-element.30), channel_id=1, source_target_pairs={{0,1},{1,0},{2,3},{3,2},{4,5},{5,4},{6,7},{7,6},{8,9},{9,8},{10,11... | collective-permute-start | bytes 3145736 | tf_op jit(solution)/shard_map/ppermute | solution.py:42
  210.4 105.6 %collective-permute-start.30 = (bf16[512,1024]{1,0:T(8,128)(2,1)S(1)}, bf16[512,1024]{1,0:T(8,128)(2,1)}, u32[]{:S(2)}, u32[]{:S(2)}) collective-permute-start(bf16[512,1024]{1,0:T(8,128)(2,1)S(1)} %get-tuple-element.28), channel_id=1, source_target_pairs={{0,12},{1,13},{2,14},{3,15},{4,8},{5,9},{6,10},{7,11},{8,4},{9,5},... | collective-permute-start | bytes 3145736 | tf_op jit(solution)/shard_map/ppermute | solution.py:42
  304.5 96.0 %collective-permute-start.1 = (bf16[4,16,1024]{2,1,0:T(8,128)(2,1)S(1)}, bf16[4,16,1024]{2,1,0:T(8,128)(2,1)S(1)}, u32[]{:S(2)}, u32[]{:S(2)}) collective-permute-start(bf16[4,16,1024]{2,1,0:T(8,128)(2,1)S(1)} %copy-done.31), channel_id=1, source_target_pairs={{0,112},{1,113},{2,114},{3,115},{4,116},{5,117},{6,118},{7,119},{8... | collective-permute-start | bytes 393224 | tf_op jit(solution)/shard_map/ppermute | solution.py:57
  306.3 94.2 %collective-permute-start.2 = (bf16[4,16,1024]{2,1,0:T(8,128)(2,1)S(1)}, bf16[4,16,1024]{2,1,0:T(8,128)(2,1)S(1)}, u32[]{:S(2)}, u32[]{:S(2)}) collective-permute-start(bf16[4,16,1024]{2,1,0:T(8,128)(2,1)S(1)} %copy-done.30), channel_id=1, source_target_pairs={{0,127},{1,112},{2,113},{3,114},{4,115},{5,116},{6,117},{7,118},{8... | collective-permute-start | bytes 393224 | tf_op jit(solution)/shard_map/ppermute | solution.py:57
  314.2 13.7 %collective-permute-start.45 = (bf16[256,1024]{1,0:T(8,128)(2,1)S(1)}, bf16[256,1024]{1,0:T(8,128)(2,1)S(1)}, u32[]{:S(2)}, u32[]{:S(2)}) collective-permute-start(bf16[256,1024]{1,0:T(8,128)(2,1)S(1)} %slice.287), channel_id=1, source_target_pairs={{0,4},{1,5},{2,6},{3,7},{4,0},{5,1},{6,2},{7,3},{8,12},{9,13},{10,... | collective-permute-start | bytes 1572872 | tf_op jit(solution)/shard_map/ppermute | solution.py:42
  316.0 13.7 %collective-permute-start.40 = (bf16[256,1024]{1,0:T(8,128)(2,1)S(1)}, bf16[256,1024]{1,0:T(8,128)(2,1)S(1)}, u32[]{:S(2)}, u32[]{:S(2)}) collective-permute-start(bf16[256,1024]{1,0:T(8,128)(2,1)S(1)} %slice.281), channel_id=1, source_target_pairs={{0,1},{1,0},{2,3},{3,2},{4,5},{5,4},{6,7},{7,6},{8,9},{9,8},{10,11... | collective-permute-start | bytes 1572872 | tf_op jit(solution)/shard_map/ppermute | solution.py:42
  328.0 14.0 %collective-permute-start.35 = (bf16[256,1024]{1,0:T(8,128)(2,1)S(1)}, bf16[256,1024]{1,0:T(8,128)(2,1)S(1)}, u32[]{:S(2)}, u32[]{:S(2)}) collective-permute-start(bf16[256,1024]{1,0:T(8,128)(2,1)S(1)} %slice.275), channel_id=1, source_target_pairs={{0,12},{1,13},{2,14},{3,15},{4,8},{5,9},{6,10},{7,11},{8,4},{9,5},... | collective-permute-start | bytes 1572872 | tf_op jit(solution)/shard_map/ppermute | solution.py:42
  329.7 14.0 %collective-permute-start.31 = (bf16[256,1024]{1,0:T(8,128)(2,1)S(1)}, bf16[256,1024]{1,0:T(8,128)(2,1)S(1)}, u32[]{:S(2)}, u32[]{:S(2)}) collective-permute-start(bf16[256,1024]{1,0:T(8,128)(2,1)S(1)} %slice.269), channel_id=1, source_target_pairs={{0,3},{1,2},{2,1},{3,0},{4,7},{5,6},{6,5},{7,4},{8,11},{9,10},{10,... | collective-permute-start | bytes 1572872 | tf_op jit(solution)/shard_map/ppermute | solution.py:42
  341.9 6.2 %collective-permute-start.46 = (bf16[128,1024]{1,0:T(8,128)(2,1)S(1)}, bf16[128,1024]{1,0:T(8,128)(2,1)S(1)}, u32[]{:S(2)}, u32[]{:S(2)}) collective-permute-start(bf16[128,1024]{1,0:T(8,128)(2,1)S(1)} %slice.289), channel_id=1, source_target_pairs={{0,1},{1,0},{2,3},{3,2},{4,5},{5,4},{6,7},{7,6},{8,9},{9,8},{10,11... | collective-permute-start | bytes 786440 | tf_op jit(solution)/shard_map/ppermute | solution.py:42
  343.7 7.4 %collective-permute-start.41 = (bf16[128,1024]{1,0:T(8,128)(2,1)S(1)}, bf16[128,1024]{1,0:T(8,128)(2,1)S(1)}, u32[]{:S(2)}, u32[]{:S(2)}) collective-permute-start(bf16[128,1024]{1,0:T(8,128)(2,1)S(1)} %slice.283), channel_id=1, source_target_pairs={{0,12},{1,13},{2,14},{3,15},{4,8},{5,9},{6,10},{7,11},{8,4},{9,5},... | collective-permute-start | bytes 786440 | tf_op jit(solution)/shard_map/ppermute | solution.py:42
  348.1 6.4 %collective-permute-start.36 = (bf16[128,1024]{1,0:T(8,128)(2,1)S(1)}, bf16[128,1024]{1,0:T(8,128)(2,1)S(1)}, u32[]{:S(2)}, u32[]{:S(2)}) collective-permute-start(bf16[128,1024]{1,0:T(8,128)(2,1)S(1)} %slice.277), channel_id=1, source_target_pairs={{0,3},{1,2},{2,1},{3,0},{4,7},{5,6},{6,5},{7,4},{8,11},{9,10},{10,... | collective-permute-start | bytes 786440 | tf_op jit(solution)/shard_map/ppermute | solution.py:42
  351.1 7.2 %collective-permute-start.32 = (bf16[128,1024]{1,0:T(8,128)(2,1)S(1)}, bf16[128,1024]{1,0:T(8,128)(2,1)S(1)}, u32[]{:S(2)}, u32[]{:S(2)}) collective-permute-start(bf16[128,1024]{1,0:T(8,128)(2,1)S(1)} %slice.271), channel_id=1, source_target_pairs={{0,4},{1,5},{2,6},{3,7},{4,0},{5,1},{6,2},{7,3},{8,12},{9,13},{10,... | collective-permute-start | bytes 786440 | tf_op jit(solution)/shard_map/ppermute | solution.py:42
  354.6 100.5 %collective-permute-start.53 = (f32[4,256,1024]{2,1,0:T(8,128)}, f32[4,256,1024]{2,1,0:T(8,128)}, u32[]{:S(2)}, u32[]{:S(2)}) collective-permute-start(f32[4,256,1024]{2,1,0:T(8,128)} %slice.247), channel_id=1, source_target_pairs={{0,16},{16,0},{32,48},{48,32},{64,80},{80,64},{96,112},{112,96},{1... | collective-permute-start | bytes 12582920 | tf_op jit(solution)/shard_map/ppermute | solution.py:42
  390.9 71.1 %collective-permute-start.52 = (f32[4,1024,256]{2,1,0:T(8,128)}, f32[4,1024,256]{2,1,0:T(8,128)}, u32[]{:S(2)}, u32[]{:S(2)}) collective-permute-start(f32[4,1024,256]{2,1,0:T(8,128)} %slice.245), channel_id=1, source_target_pairs={{0,16},{16,0},{32,48},{48,32},{64,80},{80,64},{96,112},{112,96},{1... | collective-permute-start | bytes 12582920 | tf_op jit(solution)/shard_map/ppermute | solution.py:42
  443.7 10.1 %collective-permute-start.49 = (bf16[4,16,1024]{2,1,0:T(8,128)(2,1)S(1)}, bf16[4,16,1024]{2,1,0:T(8,128)(2,1)S(1)}, u32[]{:S(2)}, u32[]{:S(2)}) collective-permute-start(bf16[4,16,1024]{2,1,0:T(8,128)(2,1)S(1)} %get-tuple-element.75), channel_id=1, source_target_pairs={{0,17},{1,18},{2,19},{3,20},{4,21},{5,22},{6,23},{7,24},{8,25},{9,... | collective-permute-start | bytes 393224 | tf_op jit(solution)/shard_map/ppermute | solution.py:57
  443.8 10.1 %collective-permute-start.50 = (bf16[4,16,1024]{2,1,0:T(8,128)(2,1)S(1)}, bf16[4,16,1024]{2,1,0:T(8,128)(2,1)S(1)}, u32[]{:S(2)}, u32[]{:S(2)}) collective-permute-start(bf16[4,16,1024]{2,1,0:T(8,128)(2,1)S(1)} %get-tuple-element.78), channel_id=1, source_target_pairs={{0,16},{1,17},{2,18},{3,19},{4,20},{5,21},{6,22},{7,23},{8,24},{9,... | collective-permute-start | bytes 393224 | tf_op jit(solution)/shard_map/ppermute | solution.py:57
  443.8 10.2 %collective-permute-start.51 = (bf16[4,16,1024]{2,1,0:T(8,128)(2,1)S(1)}, bf16[4,16,1024]{2,1,0:T(8,128)(2,1)S(1)}, u32[]{:S(2)}, u32[]{:S(2)}) collective-permute-start(bf16[4,16,1024]{2,1,0:T(8,128)(2,1)S(1)} %get-tuple-element.77), channel_id=1, source_target_pairs={{0,1},{1,2},{2,3},{3,4},{4,5},{5,6},{6,7},{7,8},{8,9},{9,10},{10,1... | collective-permute-start | bytes 393224 | tf_op jit(solution)/shard_map/ppermute | solution.py:57
  (45 other events, 424.8 us)
Sparse Core Ops, SparseCore 0:
  57.4 81.3 all-gather.1
